TPU v7x, 32 devices: a whole 2x2x4 slice. The times are simulated.
32 devices in a mesh: fsdp: 16 (over z, x, core), dp: 2 (over y).
Axes of the slice: x: 2, y: 2, z: 4, core: 2. Of those that a mesh axis runs over, the one named last changes fastest.
Arguments:
- projected: bfloat16 [20480, 4992], P(('fsdp', 'dp')), may hold values from -24 to 24
- cotangent: bfloat16 [20480, 3200], P(('fsdp', 'dp')), may hold values from -6 to 6
- out_weight: float32 [1664, 3200], P('fsdp'), may hold values from -0.15625 to 0.15625
- clip_counts: int32 [64], P(('fsdp', 'dp')), may hold values from 192 to 320, as said below
- tube_index: int32 [20480], P(('fsdp', 'dp')), may hold values from 0 to 2047, as said below
Outputs:
- out_rows: bfloat16 [20480, 3200], P(('fsdp', 'dp'))
- grad_projected: bfloat16 [20480, 4992], P(('fsdp', 'dp'))
- grad_weight: float32 [1664, 3200], P('fsdp')
Inputs may be any that keep to these rules, and one draw needn't show every extreme that they name: `clip_counts`: entry b * 2 + j counts the visible tubes of clip j of row block b. Row blocks 2p and 2p+1 together hold at most 1024 visible tubes, and some such pair holds exactly 1024; some clip holds 320. `tube_index`: within a clip the kept tube indices are distinct and ascending; a block's clips stand end to end from the block's first row, and rows after a block's last visible tube hold 0.
All inputs are finite; a program needn't handle non-finite values.
Results may differ from a plain program's by a relative error of at most 0.0018.
The roundings to bfloat16 on the way count: a program that leaves them out, or rounds other values in their place, can miss the bound.
Values may be sent and summed in bfloat16 or wider, within the bound.
A program may use at most 192 MiB of HBM per device.

v0:
```python
import jax
import jax.numpy as jnp
import numpy as np
from jax import lax
from jax.sharding import PartitionSpec as P

HS = 128
GRID = 16


HALF = 64


def pair_table():
    index = np.arange(HALF)
    first = index < 16
    second = (index >= 16) & (index < 40)
    exponent = np.where(
        first, index / 16.0, np.where(second, (index - 16) / 24.0, (index - 40) / 24.0)
    )
    which = np.where(first, 0, np.where(second, 1, 2))
    return (100.0 ** (-exponent), which)


def angles(tube_index):
    frequency, which = pair_table()
    temporal = tube_index // (GRID * GRID)
    vertical = tube_index // GRID % GRID
    lateral = tube_index % GRID
    coords = jnp.stack([temporal, vertical, lateral], axis=1).astype(jnp.float32)
    angle = coords[:, which] * jnp.asarray(frequency, dtype=jnp.float32)[None, :]
    return (jnp.cos(angle)[:, None, :], jnp.sin(angle)[:, None, :])


def rotate(values, cosine, sine):
    first = values[..., :HALF].astype(jnp.float32)
    second = values[..., HALF:].astype(jnp.float32)
    return jnp.concatenate(
        [first * cosine - second * sine, second * cosine + first * sine], axis=-1
    )


def unrotate(grads, cosine, sine):
    first = grads[..., :HALF]
    second = grads[..., HALF:]
    return jnp.concatenate(
        [first * cosine + second * sine, second * cosine - first * sine], axis=-1
    )


def softmax_rows(query_one, keys_one, same_clip, scale):
    scores = jnp.dot(query_one, keys_one.T, preferred_element_type=jnp.float32) * scale
    scores = jnp.where(same_clip, scores, -1e30)
    row_top = jnp.max(scores, axis=1, keepdims=True)
    lifted = jnp.exp(scores - row_top)
    return lifted / jnp.sum(lifted, axis=1, keepdims=True)


def body(projected, cotangent, out_weight, clip_counts, tube_index):
    row_count = projected.shape[0]
    head_width = projected.shape[1] // 3
    heads = head_width // HS
    scale = HS ** (-0.5)
    bounds = jnp.cumsum(clip_counts)
    place = jnp.arange(row_count)
    clip_of = jnp.sum((place[:, None] >= bounds[None, :]).astype(jnp.int32), axis=1)
    live = clip_of < clip_counts.shape[0]
    same_clip = clip_of[:, None] == clip_of[None, :]
    live_float = live.astype(jnp.float32)
    live_rows = live.astype(jnp.bfloat16)[:, None]
    cosine, sine = angles(tube_index)
    query = rotate(projected[:, :head_width].reshape(row_count, heads, HS), cosine, sine).astype(
        jnp.bfloat16
    )
    keys = rotate(
        projected[:, head_width : 2 * head_width].reshape(row_count, heads, HS), cosine, sine
    ).astype(jnp.bfloat16)
    values = projected[:, 2 * head_width :].reshape(row_count, heads, HS)
    query_heads = jnp.swapaxes(query, 0, 1)
    keys_heads = jnp.swapaxes(keys, 0, 1)
    values_heads = jnp.swapaxes(values, 0, 1)

    def head_forward(operands):
        query_one, keys_one, values_one = operands
        probs = softmax_rows(query_one, keys_one, same_clip, scale)
        mixed = jnp.dot(probs.astype(jnp.bfloat16), values_one, preferred_element_type=jnp.float32)
        return (mixed * live_float[:, None]).astype(jnp.bfloat16)

    attn = jnp.swapaxes(
        lax.map(head_forward, (query_heads, keys_heads, values_heads)), 0, 1
    ).reshape(row_count, head_width)
    masked_cot = cotangent * live_rows
    weight_copy = out_weight.astype(jnp.bfloat16)
    full_weight = lax.all_gather(weight_copy, "fsdp", axis=0, tiled=True)
    work_out = jnp.dot(attn, full_weight, preferred_element_type=jnp.float32).astype(jnp.bfloat16)
    work_grad = jnp.dot(masked_cot, full_weight.T, preferred_element_type=jnp.float32).astype(
        jnp.bfloat16
    )
    shard = lax.psum_scatter(
        lax.dot_general(
            attn, masked_cot, (((0,), (0,)), ((), ())), preferred_element_type=jnp.float32
        ),
        "fsdp",
        scatter_dimension=0,
        tiled=True,
    )
    grad_weight = lax.psum(shard, "dp")
    grad_heads = jnp.swapaxes(work_grad.reshape(row_count, heads, HS), 0, 1)

    def head_backward(operands):
        query_one, keys_one, values_one, grad_one = operands
        probs = softmax_rows(query_one, keys_one, same_clip, scale)
        probs_low = probs.astype(jnp.bfloat16)
        grad_values = jnp.dot(probs_low.T, grad_one, preferred_element_type=jnp.float32).astype(
            jnp.bfloat16
        )
        grad_probs = jnp.dot(grad_one, values_one.T, preferred_element_type=jnp.float32)
        centre = jnp.sum(probs * grad_probs, axis=1, keepdims=True)
        grad_scores = (probs * (grad_probs - centre) * scale).astype(jnp.bfloat16)
        grad_query = jnp.dot(grad_scores, keys_one, preferred_element_type=jnp.float32)
        grad_keys = jnp.dot(grad_scores.T, query_one, preferred_element_type=jnp.float32)
        return (grad_query, grad_keys, grad_values)

    grad_query, grad_keys, grad_values = lax.map(
        head_backward, (query_heads, keys_heads, values_heads, grad_heads)
    )
    grad_query = (
        unrotate(jnp.swapaxes(grad_query, 0, 1), cosine, sine)
        .astype(jnp.bfloat16)
        .reshape(row_count, head_width)
    )
    grad_keys = (
        unrotate(jnp.swapaxes(grad_keys, 0, 1), cosine, sine)
        .astype(jnp.bfloat16)
        .reshape(row_count, head_width)
    )
    grad_values = jnp.swapaxes(grad_values, 0, 1).reshape(row_count, head_width)
    grad_projected = jnp.concatenate([grad_query, grad_keys, grad_values], axis=1)
    return (work_out, grad_projected, grad_weight)


def solution(mesh):
    placed = (
        P(("fsdp", "dp"), None),
        P(("fsdp", "dp"), None),
        P("fsdp", None),
        P(("fsdp", "dp")),
        P(("fsdp", "dp")),
    )
    return jax.shard_map(
        body,
        mesh=mesh,
        in_specs=placed,
        out_specs=(P(("fsdp", "dp"), None), P(("fsdp", "dp"), None), P("fsdp", None)),
        check_vma=False,
    )
```

profile of v0, /device:TPU:0, one launch (start us, length us, event | category | flops | bytes accessed | tf_op | source)
XLA Modules:
  0.0 381.2 jit_solution(12887283716565589325)
XLA Ops:
  7.2 2.2 convert_element_type.71
  9.6 5.4 %fusion.67 = (bf16[640,1664]{1,0:T(8,128)(2,1)S(1)}, bf16[640,1664]{1,0:T(8,128)(2,1)}, bf16[640,1664]{1,0:T(8,128)(2,1)}) fusion(bf16[640,4992]{1,0:T(8,128)(2,1)} %param.12), kind=kLoop, calls=%fused_computation.112 | loop fusion | bytes 12779520 | tf_op jit(solution)/shard_map/slice | solution.py:78
  15.0 4.1 %copy.75 = bf16[640,1664]{0,1:T(8,128)(2,1)} copy(bf16[640,1664]{1,0:T(8,128)(2,1)} %get-tuple-element.229) | data formatting | bytes 4259840
  19.1 4.1 %copy.74 = bf16[640,1664]{0,1:T(8,128)(2,1)} copy(bf16[640,1664]{1,0:T(8,128)(2,1)} %get-tuple-element.230) | data formatting | bytes 4259840
  24.6 3.6 fusion.54
  28.2 2.4 maximum_bitcast_fusion
  30.6 4.1 %copy.52 = bf16[13,640,128]{2,1,0:T(8,128)(2,1)} copy(bf16[13,640,128]{1,2,0:T(8,128)(2,1)} %get-tuple-element.248) | data formatting | bytes 4259840
  34.7 4.1 %copy.53 = bf16[13,640,128]{2,1,0:T(8,128)(2,1)} copy(bf16[13,640,128]{1,2,0:T(8,128)(2,1)} %get-tuple-element.249) | data formatting | bytes 4259840
  38.8 2.4 copy.76
  41.2 3.3 copy.54
  46.4 38.8 %while.26 = (s32[]{:T(128)}, bf16[13,640,128]{1,2,0:T(8,128)(2,1)}, bf16[13,640,128]{2,1,0:T(8,128)(2,1)}, bf16[13,640,128]{2,1,0:T(8,128)(2,1)}, bf16[13,640,12...) while((s32[]{:T(128)}, bf16[13,640,128]{1,2,0:T(8,128)(2,1)}, ...), condition=%wide.region_5.6_spmd.clone, body=%wide.region_2.5_spmd.clone.sunk | while | flops 213564160 | bytes 6255205 | solution.py:90
  85.2 16.2 %fusion.42 = f32[1664,3200]{1,0:T(8,128)} fusion(bf16[640,1664]{0,1:T(8,128)(2,1)} %bitcast.131, bf16[640,3200]{1,0:T(8,128)(2,1)} %param.13, bf16[640]{0:T(1024)(128)(2,1)S(1)} %get-tuple-element.220), kind=kOutput, calls=%fused_computation.55 | convolution fusion | flops 6817792000 | bytes 27526400 | tf_op jit(solution)/shard_map/dot_general | solution.py:100
  102.4 12.9 %fusion.46 = bf16[640,1664]{1,0:T(8,128)(2,1)S(1)} fusion(bf16[1664,3200]{1,0:T(8,128)(2,1)} %all-gather.2.cloned.1.call-done, bf16[640,3200]{1,0:T(8,128)(2,1)} %param.13, bf16[640]{0:T(1024)(128)(2,1)S(1)} %get-tuple-element.220), kind=kOutput, calls=%fused_computation.59 | convolution fusion | flops 6818856960 | bytes 16876800 | tf_op jit(solution)/shard_map/dot_general | solution.py:96
  115.3 2.5 copy.56
  118.0 120.1 %while.27 = (s32[]{:T(128)}, f32[13,640,128]{1,2,0:T(8,128)}, f32[13,640,128]{1,2,0:T(8,128)}, bf16[13,640,128]{1,2,0:T(8,128)(2,1)S(1)}, bf16[13,640,128]{2,1,0...) while((s32[]{:T(128)}, f32[13,640,128]{1,2,0:T(8,128)}, ...), condition=%wide.region_10.11_spmd.clone, body=%wide.region_6.10_spmd.clone.sunk | while | flops 532150400 | bytes 16588405 | solution.py:124
  121.8 2.1 fusion.101
  123.9 2.0 fusion.102
  133.3 2.1 fusion.102
  149.8 2.1 fusion.101
  151.9 2.1 fusion.102
  179.4 2.1 fusion.102
  188.6 2.1 fusion.102
  197.8 2.1 fusion.102
  207.0 2.1 fusion.102
  234.5 2.1 fusion.102
  238.1 4.9 %add_convert_fusion.1 = (bf16[640,13,64]{0,2,1:T(8,128)(2,1)S(1)}, bf16[640,13,64]{0,2,1:T(8,128)(2,1)S(1)}, bf16[640,13,64]{0,2,1:T(8,128)(2,1)S(1)}, bf16[640,13,64]{0,2,1:T(8,128)(2,1)S(1)}) fusion(f32[640,13,128]{0,2,1:T(8,128)} %bitcast.128, f32[640,64]{0,1:T(8,128)S(1)} %get-tuple-element.244, f32[640,64]{0,1:T(8,128)S(1)} %get-tuple-element.243, ...), kind=kLoop, calls=%fused_computation.83 | loop fusion | flops 8519680 | bytes 13107200 | tf_op jit(solution)/shard_map/convert.2
  246.0 5.5 %pad_maximum_fusion = bf16[640,4992]{0,1:T(8,128)(2,1)} fusion(bf16[640,1664]{0,1:T(8,128)(2,1)S(1)} %bitcast.122, bf16[640,1664]{0,1:T(8,128)(2,1)} %bitcast.123, bf16[640,1664]{0,1:T(8,128)(2,1)} %bitcast.124), kind=kLoop, calls=%fused_computation.53 | loop fusion | flops 19169280 | bytes 12779520 | tf_op jit(solution)/shard_map/concatenate | solution.py:138
  251.5 9.7 %copy.64 = bf16[640,4992]{1,0:T(8,128)(2,1)} copy(bf16[640,4992]{0,1:T(8,128)(2,1)} %pad_maximum_fusion) | data formatting | bytes 12779520
  261.3 63.3 %reduce-scatter.4.cloned.1.call-done = f32[104,3200]{1,0:T(8,128)} async-done(((f32[1664,3200]{1,0:T(8,128)}), f32[104,3200]{1,0:T(8,128)}) %reduce-scatter.4.cloned.1.call-update) | async-done | bytes 1331216
  324.6 12.8 %convolution_convert_fusion.1 = bf16[640,3200]{1,0:T(8,128)(2,1)} fusion(bf16[640,1664]{0,1:T(8,128)(2,1)S(1)} %bitcast.132, bf16[1664,3200]{1,0:T(8,128)(2,1)} %all-gather.2.cloned.1.call-done), kind=kOutput, calls=%fused_computation.54 | convolution fusion | flops 6817792000 | bytes 16875520 | tf_op jit(solution)/shard_map/dot_general | solution.py:95
  337.4 34.9 %all-reduce.3.cloned.1.call-done = f32[104,3200]{1,0:T(8,128)} async-done(((f32[104,3200]{1,0:T(8,128)}), f32[104,3200]{1,0:T(8,128)}) %all-reduce.3.cloned.1.call-update) | async-done | bytes 1331216 | tf_op jit(solution)/shard_map/psum | solution.py:107
  372.2 2.5 copy.105
  (209 shorter events, 145.1 us)
Async XLA Ops:
  7.2 2.4 copy-start.2
  7.2 95.2 %all-gather.2.cloned.1.call-start = ((), (), s32[]{:S(2)}) async-start(), calls=%async_computation.1 | async-start | bytes 11315200 | tf_op jit(solution)/shard_map/all_gather | solution.py:94
  9.5 315.1 %reduce-scatter.4.cloned.1.call-start = ((), (), s32[]{:S(2)}) async-start(), calls=%async_computation.3 | async-start | bytes 22630400
  19.1 4.1 %copy-start.4 = (s32[64]{0:T(128)S(1)}, s32[64]{0:T(128)}, u32[]{:S(2)}) copy-start(s32[64]{0:T(128)} %constant.108) | copy-start | bytes 772
  23.2 0.7 copy-start.3
  41.2 3.4 copy-start.5
  85.2 16.2 %copy-start = (bf16[13,640,128]{2,1,0:T(8,128)(2,1)}, bf16[13,640,128]{2,1,0:T(8,128)(2,1)S(1)}, u32[]{:S(2)}) copy-start(bf16[13,640,128]{2,1,0:T(8,128)(2,1)S(1)} %get-tuple-element.426) | copy-start | bytes 6389764
  101.4 270.8 %all-reduce.3.cloned.1.call-start = ((), (), s32[]{:S(2)}) async-start(), calls=%async_computation.2 | async-start | bytes 2662400 | tf_op jit(solution)/shard_map/psum | solution.py:107
  251.5 73.1 %copy-start.1 = (bf16[13,640,128]{1,2,0:T(8,128)(2,1)S(1)}, bf16[13,640,128]{1,2,0:T(8,128)(2,1)}, u32[]{:S(2)}) copy-start(bf16[13,640,128]{1,2,0:T(8,128)(2,1)} %get-tuple-element.89) | copy-start | bytes 6389764
Sparse Core Ops, SparseCore 0:
  10.7 91.6 all-gather.1
  106.4 218.1 reduce-scatter.3
  326.9 45.3 all-reduce.2
where the time goes:
time: 384 us; the launch traced here: 381 us
  matrix products  174 us (45%)
  waiting for transfers between devices  99 us (26%)
  local copies, waits for them, and re-layouts  58.2 us (15%)
  other arithmetic  35.3 us (9%)
  between operations  13.9 us (4%)
    unnamed x4, waiting for transfers between devices  63.4 us
    dot_general x26, matrix products, softmax_rows(): jnp.dot(query_one, keys_one.T, preferred_element_type=jnp.float32) * scale  37.2 us
    psum x1, waiting for transfers between devices, body(): grad_weight = lax.psum(shard, 'dp')  34.9 us
    unnamed x20, local copies, waits for them, and re-layouts  34.3 us
    dot_general x13, matrix products, head_backward(): jnp.dot(grad_scores.T, query_one, preferred_element_type=jnp.float32)  26.6 us
    dot_general x13, matrix products, head_backward(): jnp.dot(grad_scores, keys_one, preferred_element_type=jnp.float32)  26.3 us
    dot_general x13, matrix products, head_backward(): jnp.dot(grad_one, values_one.T, preferred_element_type=jnp.float32)  18.8 us
    dot_general x13, matrix products, head_backward(): jnp.dot(probs_low.T, grad_one, preferred_element_type=jnp.float32)  17.4 us
  transfers between devices with their start and end apart: 3, of which 3 were waited for; matrix products, arithmetic and copies ran while one was open for 69% of the time, Pallas kernels for 0%

commit v1 on v0

v1 whole, which is shorter than its diff:
```python
import jax
import jax.numpy as jnp
import numpy as np
from jax import lax
from jax.experimental import pallas as pl
from jax.experimental.pallas import tpu as pltpu
from jax.sharding import PartitionSpec as P

HS = 128
GRID = 16
HALF = 64
CHUNKS = 5
NEG = -1e30
VMEM_BYTES = 48 * 1024 * 1024


def pair_table():
    index = np.arange(HALF)
    first = index < 16
    second = (index >= 16) & (index < 40)
    exponent = np.where(
        first, index / 16.0, np.where(second, (index - 16) / 24.0, (index - 40) / 24.0)
    )
    which = np.where(first, 0, np.where(second, 1, 2))
    return (100.0 ** (-exponent), which)


def angles(tube_index):
    frequency, which = pair_table()
    temporal = (tube_index // (GRID * GRID)).astype(jnp.float32)[:, None]
    vertical = (tube_index // GRID % GRID).astype(jnp.float32)[:, None]
    lateral = (tube_index % GRID).astype(jnp.float32)[:, None]
    which = jnp.asarray(which)[None, :]
    coords = jnp.where(which == 0, temporal, jnp.where(which == 1, vertical, lateral))
    angle = coords * jnp.asarray(frequency, dtype=jnp.float32)[None, :]
    cosine, sine = jnp.cos(angle), jnp.sin(angle)
    return (
        jnp.concatenate([cosine, cosine], axis=1),
        jnp.concatenate([-sine, sine], axis=1),
    )


def rotate(values, cosine, sine):
    wide = values.astype(jnp.float32)
    return wide * cosine + pltpu.roll(wide, HALF, 1) * sine


def unrotate(grads, cosine, sine):
    return grads * cosine - pltpu.roll(grads, HALF, 1) * sine


def windows(counts_ref, rows):
    first, second = counts_ref[0], counts_ref[1]
    half = rows // 2
    wide = half + 16
    start = jnp.minimum(first // 16 * 16, rows - wide)
    return (
        (0, half, 0, first),
        (pl.multiple_of(start, 16), wide, first, first + second),
    )


def probs_t(keys, query, start, low, high, scale):
    scores = (
        lax.dot_general(
            keys, query, (((1,), (1,)), ((), ())), preferred_element_type=jnp.float32
        )
        * scale
    )
    place = start + lax.broadcasted_iota(jnp.int32, (keys.shape[0], 1), 0)
    scores = jnp.where((place >= low) & (place < high), scores, NEG)
    lifted = jnp.exp(scores - jnp.max(scores, axis=0, keepdims=True))
    return lifted * (1.0 / jnp.sum(lifted, axis=0, keepdims=True))


def forward_kernel(
    counts_ref, q_ref, k_ref, v_ref, cos_ref, sin_ref, out_ref, qr, kr, total
):
    rows = q_ref.shape[0]
    scale = HS ** (-0.5)
    cosine, sine = cos_ref[...], sin_ref[...]
    qr[...] = rotate(q_ref[...], cosine, sine).astype(jnp.bfloat16)
    kr[...] = rotate(k_ref[...], cosine, sine).astype(jnp.bfloat16)
    total[...] = jnp.zeros_like(total)
    for start, wide, low, high in windows(counts_ref, rows):
        span = pl.ds(start, wide)
        probs = probs_t(kr[span, :], qr[span, :], start, low, high, scale)
        mixed = lax.dot_general(
            v_ref[span, :],
            probs.astype(jnp.bfloat16),
            (((0,), (0,)), ((), ())),
            preferred_element_type=jnp.float32,
        ).T
        place = start + lax.broadcasted_iota(jnp.int32, (wide, 1), 0)
        total[span, :] += jnp.where((place >= low) & (place < high), mixed, 0.0)
    out_ref[...] = total[...].T.astype(jnp.bfloat16)


def backward_kernel(
    counts_ref, q_ref, k_ref, v_ref, g_ref, cos_ref, sin_ref, out_ref, qr, kr, go, total, low_out
):
    part = pl.program_id(1)

    @pl.when(part == 0)
    def _():
        rows = q_ref.shape[0]
        scale = HS ** (-0.5)
        cosine, sine = cos_ref[...], sin_ref[...]
        qr[...] = rotate(q_ref[...], cosine, sine).astype(jnp.bfloat16)
        kr[...] = rotate(k_ref[...], cosine, sine).astype(jnp.bfloat16)
        go[...] = g_ref[...].astype(jnp.float32).T.astype(jnp.bfloat16)
        total[...] = jnp.zeros_like(total)
        for start, wide, low, high in windows(counts_ref, rows):
            span = pl.ds(start, wide)
            keys, query, values = kr[span, :], qr[span, :], v_ref[span, :]
            place = start + lax.broadcasted_iota(jnp.int32, (wide, 1), 0)
            grad = jnp.where(
                (place >= low) & (place < high), go[span, :].astype(jnp.float32), 0.0
            ).astype(jnp.bfloat16)
            probs = probs_t(keys, query, start, low, high, scale)
            total[2, span, :] += jnp.dot(
                probs.astype(jnp.bfloat16), grad, preferred_element_type=jnp.float32
            )
            grad_probs = lax.dot_general(
                values, grad, (((1,), (1,)), ((), ())), preferred_element_type=jnp.float32
            )
            centre = jnp.sum(probs * grad_probs, axis=0, keepdims=True)
            grad_scores = (probs * (grad_probs - centre) * scale).astype(jnp.bfloat16)
            total[1, span, :] += jnp.dot(grad_scores, query, preferred_element_type=jnp.float32)
            total[0, span, :] += lax.dot_general(
                keys, grad_scores, (((0,), (0,)), ((), ())), preferred_element_type=jnp.float32
            ).T
        low_out[0] = unrotate(total[0], cosine, sine).astype(jnp.bfloat16)
        low_out[1] = unrotate(total[1], cosine, sine).astype(jnp.bfloat16)
        low_out[2] = total[2].astype(jnp.bfloat16)

    out_ref[...] = low_out[part]


def attention_forward(projected, clip_counts, cosine, sine):
    rows = projected.shape[0]
    heads = projected.shape[1] // 3 // HS
    whole = pl.BlockSpec((rows, HS), lambda h, c: (0, 0))
    return pl.pallas_call(
        forward_kernel,
        grid_spec=pltpu.PrefetchScalarGridSpec(
            num_scalar_prefetch=1,
            grid=(heads,),
            in_specs=[
                pl.BlockSpec((rows, HS), lambda h, c: (0, h)),
                pl.BlockSpec((rows, HS), lambda h, c: (0, h + heads)),
                pl.BlockSpec((rows, HS), lambda h, c: (0, h + 2 * heads)),
                whole,
                whole,
            ],
            out_specs=pl.BlockSpec((HS, rows), lambda h, c: (h, 0)),
            scratch_shapes=[
                pltpu.VMEM((rows, HS), jnp.bfloat16),
                pltpu.VMEM((rows, HS), jnp.bfloat16),
                pltpu.VMEM((rows, HS), jnp.float32),
            ],
        ),
        out_shape=jax.ShapeDtypeStruct((heads * HS, rows), jnp.bfloat16),
        compiler_params=pltpu.CompilerParams(vmem_limit_bytes=VMEM_BYTES),
        cost_estimate=pl.CostEstimate(
            flops=heads * rows * rows * HS * 6, bytes_accessed=rows * heads * HS * 8,
            transcendentals=heads * rows * rows,
        ),
    )(clip_counts, projected, projected, projected, cosine, sine)


def attention_backward(projected, clip_counts, grad_t, cosine, sine):
    rows = projected.shape[0]
    heads = projected.shape[1] // 3 // HS
    whole = pl.BlockSpec((rows, HS), lambda h, j, c: (0, 0))
    return pl.pallas_call(
        backward_kernel,
        grid_spec=pltpu.PrefetchScalarGridSpec(
            num_scalar_prefetch=1,
            grid=(heads, 3),
            in_specs=[
                pl.BlockSpec((rows, HS), lambda h, j, c: (0, h)),
                pl.BlockSpec((rows, HS), lambda h, j, c: (0, h + heads)),
                pl.BlockSpec((rows, HS), lambda h, j, c: (0, h + 2 * heads)),
                pl.BlockSpec((HS, rows), lambda h, j, c: (h, 0)),
                whole,
                whole,
            ],
            out_specs=pl.BlockSpec((rows, HS), lambda h, j, c: (0, j * heads + h)),
            scratch_shapes=[
                pltpu.VMEM((rows, HS), jnp.bfloat16),
                pltpu.VMEM((rows, HS), jnp.bfloat16),
                pltpu.VMEM((rows, HS), jnp.bfloat16),
                pltpu.VMEM((3, rows, HS), jnp.float32),
                pltpu.VMEM((3, rows, HS), jnp.bfloat16),
            ],
        ),
        out_shape=jax.ShapeDtypeStruct(projected.shape, jnp.bfloat16),
        compiler_params=pltpu.CompilerParams(vmem_limit_bytes=VMEM_BYTES),
        cost_estimate=pl.CostEstimate(
            flops=heads * rows * rows * HS * 14, bytes_accessed=rows * heads * HS * 14,
            transcendentals=heads * rows * rows,
        ),
    )(clip_counts, projected, projected, projected, grad_t, cosine, sine)


def body(sizes, projected, cotangent, out_weight, clip_counts, tube_index):
    devices, pair = sizes
    bits = devices.bit_length() - 1
    rows = projected.shape[0]
    head_width = projected.shape[1] // 3
    depth = out_weight.shape[0]
    width = out_weight.shape[1]
    piece = width // CHUNKS
    me = lax.axis_index("fsdp")
    row_side = lax.axis_index("dp")

    def across(array, bit):
        if bit < 0:
            return lax.ppermute(array, "dp", [(i, i ^ 1) for i in range(pair)])
        return lax.ppermute(array, "fsdp", [(i, i ^ (1 << bit)) for i in range(devices)])

    slot = np.array([int(format(i, f"0{bits}b")[::-1], 2) for i in range(devices)])

    def to_places(array):
        return jnp.concatenate(
            [
                lax.dynamic_slice_in_dim(array, (int(p) ^ me) * depth, depth, 0)
                for p in slot
            ],
            axis=0,
        )

    def from_places(array):
        table = jnp.asarray(slot, dtype=jnp.int32)
        return jnp.concatenate(
            [
                lax.dynamic_slice_in_dim(array, table[j ^ me] * depth, depth, 0)
                for j in range(devices)
            ],
            axis=0,
        )

    x_bit, z_bits = 1, list(range(2, bits))

    def gather(part, order):
        array = part.reshape((1,) * bits + part.shape)
        for bit in order:
            array = jnp.concatenate([array, across(array, bit)], axis=bit)
        return array.reshape(devices * depth, piece)

    def reduce(keep, send, order):
        array = keep + across(send, 0)
        array = array.reshape((1,) + (2,) * (bits - 1) + (depth, piece))
        for bit in order:
            if bit < 0:
                continue
            send = lax.slice_in_dim(array, 1, 2, axis=bit)
            keep = lax.slice_in_dim(array, 0, 1, axis=bit)
            array = keep + across(send, bit)
        return array.reshape(depth, piece)

    weight_copy = out_weight.astype(jnp.bfloat16)

    def columns(array, index):
        return lax.dynamic_slice_in_dim(array, index * piece, piece, 1)

    down = z_bits[::-1]
    own = gather(columns(weight_copy, row_side), [x_bit] + down + [0])
    other = across(own, -1)
    weights = [jnp.where(row_side == 0, own, other), jnp.where(row_side == 0, other, own)]
    for index in (2, 3):
        weights.append(gather(columns(weight_copy, index), down + [x_bit, 0]))
    weights.append(gather(columns(weight_copy, 4), [x_bit] + down + [0]))
    full_weight = jnp.concatenate(weights, axis=1)

    bounds = jnp.cumsum(clip_counts)
    live_rows = (jnp.arange(rows) < bounds[-1]).astype(jnp.bfloat16)[:, None]
    cosine, sine = angles(tube_index)
    masked_cot = cotangent * live_rows
    attn_t = to_places(attention_forward(projected, clip_counts, cosine, sine))
    half = head_width // 2
    keep_t, send_t = attn_t[:half], attn_t[half:]

    def product(left, index):
        return jnp.dot(left, columns(masked_cot, index), preferred_element_type=jnp.float32)

    mine, theirs = row_side, 1 - row_side
    own_keep, own_send = product(keep_t, mine), product(send_t, mine)
    other_keep, other_send = product(keep_t, theirs), product(send_t, theirs)
    pair_send = other_keep + across(other_send, 0)
    pair_keep = own_keep + across(own_send, 0)
    array = pair_keep + across(pair_send, -1)
    array = array.reshape((1,) + (2,) * (bits - 1) + (depth, piece))
    for bit in z_bits + [x_bit]:
        array = lax.slice_in_dim(array, 0, 1, axis=bit) + across(
            lax.slice_in_dim(array, 1, 2, axis=bit), bit
        )
    own = array.reshape(depth, piece)
    other = across(own, -1)
    grads = [jnp.where(row_side == 0, own, other), jnp.where(row_side == 0, other, own)]
    for index, order in ((2, [x_bit] + z_bits), (3, [x_bit] + z_bits), (4, z_bits + [x_bit])):
        own = reduce(product(keep_t, index), product(send_t, index), order)
        grads.append(own + across(own, -1))
    grad_weight = jnp.concatenate(grads, axis=1)

    grad_t = lax.dot_general(
        full_weight, masked_cot, (((1,), (1,)), ((), ())), preferred_element_type=jnp.float32
    ).astype(jnp.bfloat16)
    grad_projected = attention_backward(
        projected, clip_counts, from_places(grad_t), cosine, sine
    )
    work_out = lax.dot_general(
        attn_t, full_weight, (((0,), (0,)), ((), ())), preferred_element_type=jnp.float32
    ).astype(jnp.bfloat16)
    return (work_out, grad_projected, grad_weight)


def solution(mesh):
    placed = (
        P(("fsdp", "dp"), None),
        P(("fsdp", "dp"), None),
        P("fsdp", None),
        P(("fsdp", "dp")),
        P(("fsdp", "dp")),
    )
    sizes = (mesh.shape["fsdp"], mesh.shape["dp"])

    def local(*args):
        return body(sizes, *args)

    return jax.shard_map(
        local,
        mesh=mesh,
        in_specs=placed,
        out_specs=(P(("fsdp", "dp"), None), P(("fsdp", "dp"), None), P("fsdp", None)),
        check_vma=False,
    )
```

time: 384 us -> 368 us (0.958)
  matrix products: 174 us -> 44.9 us
  Pallas kernels: 0 us -> 72.5 us
  waiting for transfers between devices: 99 us -> 149 us
  starting transfers between devices: 0.3 us -> 40.1 us
  local copies, waits for them, and re-layouts: 58.2 us -> 21.1 us
  other arithmetic: 35.3 us -> 27.4 us
    ppermute x0 -> x39, waiting for transfers between devices: none -> 149 us  [the longest x33 149 us: across(): lax.ppermute(array, 'fsdp', [(i, i ^ 1 << bit) for i in range(devices)])]
    dot_general x94 -> x12, matrix products: 174 us -> 44.9 us  [the longest x10 23.5 us: product(): jnp.dot(left, columns(masked_cot, index), preferred_element_type=jnp.floa...]
    pallas_call x0 -> x2, Pallas kernels: none -> 72.5 us  [the longest x1 53.8 us: attention_backward(): pl.pallas_call(backward_kernel, grid_spec=pltpu.PrefetchScalarGridSpec(nu...]
    unnamed x4 -> x0, waiting for transfers between devices: 63.4 us -> none
    ppermute x0 -> x39, starting transfers between devices: none -> 40.1 us  [the longest x33 31.7 us: across(): lax.ppermute(array, 'fsdp', [(i, i ^ 1 << bit) for i in range(devices)])]
    psum x1 -> x0, waiting for transfers between devices: 34.9 us -> none  [body(): grad_weight = lax.psum(shard, 'dp')]
    unnamed x20 -> x70, local copies, waits for them, and re-layouts: 34.3 us -> 18.7 us
    dynamic_update_slice x52 -> x0, local copies, waits for them, and re-layouts: 13.5 us -> none  [body(): lax.map(head_forward, (query_heads, keys_heads, values_heads))]
  transfers between devices with their start and end apart: 3 -> 39, of which waited for: 3 -> 14; matrix products, arithmetic and copies ran while one was open for 69% -> 23% of each run, Pallas kernels for 0% -> 20%
where the time goes in v1:
time: 368 us; the launch traced here: 367 us
  waiting for transfers between devices  149 us (40%)
  Pallas kernels  72.5 us (20%)
  matrix products  44.9 us (12%)
  starting transfers between devices  40.1 us (11%)
  other arithmetic  27.4 us (7%)
  local copies, waits for them, and re-layouts  21.1 us (6%)
  between operations  11.7 us (3%)
    ppermute x33, waiting for transfers between devices, across(): lax.ppermute(array, 'fsdp', [(i, i ^ 1 << bit) for i in range(devices)])  149 us
    pallas_call x1, Pallas kernels, attention_backward(): pl.pallas_call(backward_kernel, grid_spec=pltpu.PrefetchScalarGridSpec(nu...  53.8 us
    ppermute x33, starting transfers between devices, across(): lax.ppermute(array, 'fsdp', [(i, i ^ 1 << bit) for i in range(devices)])  31.7 us
    dot_general x10, matrix products, product(): jnp.dot(left, columns(masked_cot, index), preferred_element_type=jnp.floa...  23.5 us
    pallas_call x1, Pallas kernels, attention_forward(): pl.pallas_call(forward_kernel, grid_spec=pltpu.PrefetchScalarGridSpec(num...  18.7 us
    unnamed x70, local copies, waits for them, and re-layouts  18.7 us
    concatenate x16, other arithmetic, gather(): array = jnp.concatenate([array, across(array, bit)], axis=bit)  16.2 us
    dot_general x1, matrix products, body(): lax.dot_general(attn_t, full_weight, (((0,), (0,)), ((), ())), preferred_...  12.5 us
  transfers between devices with their start and end apart: 39, of which 14 were waited for; matrix products, arithmetic and copies ran while one was open for 23% of the time, Pallas kernels for 20%

profile of v1, /device:TPU:0, one launch (start us, length us, event | category | flops | bytes accessed | tf_op | source)
XLA Modules:
  0.0 366.7 jit_solution(9970806087151338847)
XLA Ops:
  2.2 3.0 collective-permute-start
  5.2 2.6 collective-permute-start.5
  9.7 2.4 fusion.22
  12.4 18.7 %shard_map.103 = bf16[1664,640]{1,0:T(8,128)(2,1)S(1)} custom-call(s32[2]{0:T(128)S(1)} %copy-done, bf16[640,4992]{1,0:T(8,128)(2,1)} %v_ref.3, bf16[640,4992]{1,0:T(8,128)(2,1)} %v_ref.3, bf16[640,4992]{1,0:T(8,128)(2,1)} %v_ref.3, f32[640,128]{1,0:T(8,128)S(1)} %get-tuple-element.46.cos_ref, f32[640,128]{1,0:T(8,128)S(1)} %get-tuple-element.47.sin_ref), custom_call_target="tpu_custom_call" | custom-call | flops 4089446400 | bytes 8519680 | tf_op jit(solution)/shard_map/pallas_call | solution.py:144
  42.9 2.7 fusion.6
  45.6 2.5 fusion.3
  49.0 3.0 collective-permute-start.1
  56.1 8.9 %collective-permute-done.1 = bf16[1,2,1,1,104,640]{5,4,3,2,1,0:T(8,128)(2,1)S(1)} collective-permute-done((bf16[1,2,1,1,104,640]{5,4,3,2,1,0:T(8,128)(2,1)S(1)}, bf16[1,2,1,1,104,640]{5,4,3,2,1,0:T(8,128)(2,1)S(1)}, u32[]{:S(2)}, u32[]{:S(2)}) %collective-permute-start.1) | collective-permute-done | bytes 266272 | tf_op jit(solution)/shard_map/ppermute | solution.py:221
  66.6 5.9 %collective-permute-done.6 = bf16[1,1,1,2,104,640]{5,4,3,2,1,0:T(8,128)(2,1)S(1)} collective-permute-done((bf16[1,1,1,2,104,640]{5,4,3,2,1,0:T(8,128)(2,1)S(1)}, bf16[1,1,1,2,104,640]{5,4,3,2,1,0:T(8,128)(2,1)S(1)}, u32[]{:S(2)}, u32[]{:S(2)}) %collective-permute-start.6) | collective-permute-done | bytes 266272 | tf_op jit(solution)/shard_map/ppermute | solution.py:221
  75.0 2.5 fusion
  78.2 1.8 pad_maximum_fusion.10
  82.3 6.5 %collective-permute-done.2 = bf16[1,2,1,2,104,640]{5,4,3,2,1,0:T(8,128)(2,1)S(1)} collective-permute-done((bf16[1,2,1,2,104,640]{5,4,3,2,1,0:T(8,128)(2,1)S(1)}, bf16[1,2,1,2,104,640]{5,4,3,2,1,0:T(8,128)(2,1)S(1)}, u32[]{:S(2)}, u32[]{:S(2)}) %collective-permute-start.2) | collective-permute-done | bytes 532512 | tf_op jit(solution)/shard_map/ppermute | solution.py:221
  89.7 2.0 pad_maximum_fusion.4
  91.7 2.6 fusion.12
  107.2 4.2 %fusion.9 = f32[832,640]{1,0:T(8,128)} fusion(bf16[832,640]{1,0:T(8,128)(2,1)} %copy-done.10, bf16[640,3200]{1,0:T(8,128)(2,1)} %copy-done.2, s32[]{:T(128)S(6)} %select_n.263), kind=kOutput, calls=%fused_computation.31 | convolution fusion | flops 681574400 | bytes 4014084 | tf_op jit(solution)/shard_map/dot_general | solution.py:286
  117.7 2.7 convolution_add_fusion.2
  122.1 3.0 convolution_add_fusion.1
  129.9 17.1 %collective-permute-done.25 = f32[1,1,2,2,104,640]{5,4,3,2,1,0:T(8,128)S(1)} collective-permute-done((f32[1,1,2,2,104,640]{5,4,3,2,1,0:T(8,128)S(1)}, f32[1,1,2,2,104,640]{5,4,3,2,1,0:T(8,128)S(1)}, u32[]{:S(2)}, u32[]{:S(2)}) %collective-permute-start.25) | collective-permute-done | bytes 1064992 | tf_op jit(solution)/shard_map/ppermute | solution.py:221
  148.7 20.3 %collective-permute-done.30 = f32[1,1,2,2,104,640]{5,4,3,2,1,0:T(8,128)S(1)} collective-permute-done((f32[1,1,2,2,104,640]{5,4,3,2,1,0:T(8,128)S(1)}, f32[1,1,2,2,104,640]{5,4,3,2,1,0:T(8,128)S(1)}, u32[]{:S(2)}, u32[]{:S(2)}) %collective-permute-start.30) | collective-permute-done | bytes 1064992 | tf_op jit(solution)/shard_map/ppermute | solution.py:221
  171.4 2.3 collective-permute-start.36
  174.9 20.5 %collective-permute-done.26 = f32[1,1,1,2,104,640]{5,4,3,2,1,0:T(8,128)S(1)} collective-permute-done((f32[1,1,1,2,104,640]{5,4,3,2,1,0:T(8,128)S(1)}, f32[1,1,1,2,104,640]{5,4,3,2,1,0:T(8,128)S(1)}, u32[]{:S(2)}, u32[]{:S(2)}) %collective-permute-start.26) | collective-permute-done | bytes 532512 | tf_op jit(solution)/shard_map/ppermute | solution.py:221
  197.1 8.0 %collective-permute-done.31 = f32[1,1,1,2,104,640]{5,4,3,2,1,0:T(8,128)S(1)} collective-permute-done((f32[1,1,1,2,104,640]{5,4,3,2,1,0:T(8,128)S(1)}, f32[1,1,1,2,104,640]{5,4,3,2,1,0:T(8,128)S(1)}, u32[]{:S(2)}, u32[]{:S(2)}) %collective-permute-start.31) | collective-permute-done | bytes 532512 | tf_op jit(solution)/shard_map/ppermute | solution.py:221
  205.8 2.4 collective-permute-start.32
  208.3 15.7 %collective-permute-done.27 = f32[1,1,1,1,104,640]{5,4,3,2,1,0:T(8,128)S(1)} collective-permute-done((f32[1,1,1,1,104,640]{5,4,3,2,1,0:T(8,128)S(1)}, f32[1,1,1,1,104,640]{5,4,3,2,1,0:T(8,128)S(1)}, u32[]{:S(2)}, u32[]{:S(2)}) %collective-permute-start.27) | collective-permute-done | bytes 266272 | tf_op jit(solution)/shard_map/ppermute | solution.py:221
  225.5 4.1 %collective-permute-done.32 = f32[1,1,1,1,104,640]{5,4,3,2,1,0:T(8,128)S(1)} collective-permute-done((f32[1,1,1,1,104,640]{5,4,3,2,1,0:T(8,128)S(1)}, f32[1,1,1,1,104,640]{5,4,3,2,1,0:T(8,128)S(1)}, u32[]{:S(2)}, u32[]{:S(2)}) %collective-permute-start.32) | collective-permute-done | bytes 266272 | tf_op jit(solution)/shard_map/ppermute | solution.py:221
  236.8 4.1 %copy-done.7 = bf16[1664,3200]{1,0:T(8,128)(2,1)} copy-done((bf16[1664,3200]{1,0:T(8,128)(2,1)}, bf16[1664,3200]{1,0:T(8,128)(2,1)S(1)}, u32[]{:S(2)}) %copy-start.7) | copy-done | bytes 10649624
  240.9 8.9 %convolution_convert_fusion.1 = bf16[1664,640]{1,0:T(8,128)(2,1)S(1)} fusion(bf16[1664,3200]{1,0:T(8,128)(2,1)S(1)} %constant_dynamic-update-slice_fusion.16, bf16[640,3200]{1,0:T(8,128)(2,1)S(1)} %copy-done.3), kind=kOutput, calls=%fused_computation.1 | convolution fusion | flops 6816808960 | bytes 16875520 | tf_op jit(solution)/shard_map/dot_general | solution.py:307
  252.0 12.5 %convolution_convert_fusion = bf16[640,3200]{1,0:T(8,128)(2,1)} fusion(bf16[1664,640]{1,0:T(8,128)(2,1)S(1)} %copy-done.11, bf16[1664,3200]{1,0:T(8,128)(2,1)} %copy-done.7), kind=kOutput, calls=%fused_computation | convolution fusion | flops 6817792000 | bytes 16875520 | tf_op jit(solution)/shard_map/dot_general | solution.py:313
  264.5 9.9 %collective-permute-done.20 = f32[1,2,1,2,104,640]{5,4,3,2,1,0:T(8,128)S(1)} collective-permute-done((f32[1,2,1,2,104,640]{5,4,3,2,1,0:T(8,128)S(1)}, f32[1,2,1,2,104,640]{5,4,3,2,1,0:T(8,128)S(1)}, u32[]{:S(2)}, u32[]{:S(2)}) %collective-permute-start.20) | collective-permute-done | bytes 1064992 | tf_op jit(solution)/shard_map/ppermute | solution.py:221
  275.3 23.3 %collective-permute-done.21 = f32[1,2,1,1,104,640]{5,4,3,2,1,0:T(8,128)S(1)} collective-permute-done((f32[1,2,1,1,104,640]{5,4,3,2,1,0:T(8,128)S(1)}, f32[1,2,1,1,104,640]{5,4,3,2,1,0:T(8,128)S(1)}, u32[]{:S(2)}, u32[]{:S(2)}) %collective-permute-start.21) | collective-permute-done | bytes 532512 | tf_op jit(solution)/shard_map/ppermute | solution.py:221
  300.3 6.8 %collective-permute-done.22 = f32[1,1,1,1,104,640]{5,4,3,2,1,0:T(8,128)S(1)} collective-permute-done((f32[1,1,1,1,104,640]{5,4,3,2,1,0:T(8,128)S(1)}, f32[1,1,1,1,104,640]{5,4,3,2,1,0:T(8,128)S(1)}, u32[]{:S(2)}, u32[]{:S(2)}) %collective-permute-start.22) | collective-permute-done | bytes 266272 | tf_op jit(solution)/shard_map/ppermute | solution.py:221
  308.7 53.8 %shard_map.104 = bf16[640,4992]{1,0:T(8,128)(2,1)} custom-call(s32[2]{0:T(128)S(1)} %copy-done, bf16[640,4992]{1,0:T(8,128)(2,1)} %v_ref.3, bf16[640,4992]{1,0:T(8,128)(2,1)} %v_ref.3, bf16[640,4992]{1,0:T(8,128)(2,1)} %v_ref.3, bf16[1664,640]{1,0:T(8,128)(2,1)S(1)} %dynamic-slice_dynamic-update-slice_fusion.g_ref, ...), custom_call_target="tpu_custom_call" | custom-call | flops 9542041600 | bytes 14909440 | tf_op jit(solution)/shard_map/pallas_call | solution.py:176
  (191 shorter events, 70.2 us)
Async XLA Ops:
  2.2 45.9 %collective-permute-start = (bf16[1,1,1,1,104,640]{5,4,3,2,1,0:T(8,128)(2,1)S(1)}, bf16[1,1,1,1,104,640]{5,4,3,2,1,0:T(8,128)(2,1)}, u32[]{:S(2)}, u32[]{:S(2)}) collective-permute-start(bf16[1,1,1,1,104,640]{5,4,3,2,1,0:T(8,128)(2,1)S(1)} %get-tuple-element.23), channel_id=1, source_target_pairs={{0,4},{2,6},{4,0},{6,2},{8,12},{10,14},{12,8},{14,10},{16,20},{18,... | collective-permute-start | bytes 399368 | tf_op jit(solution)/shard_map/ppermute | solution.py:221
  5.2 46.8 %collective-permute-start.5 = (bf16[1,1,1,1,104,640]{5,4,3,2,1,0:T(8,128)(2,1)S(1)}, bf16[1,1,1,1,104,640]{5,4,3,2,1,0:T(8,128)(2,1)}, u32[]{:S(2)}, u32[]{:S(2)}) collective-permute-start(bf16[1,1,1,1,104,640]{5,4,3,2,1,0:T(8,128)(2,1)S(1)} %get-tuple-element.22), channel_id=1, source_target_pairs={{0,16},{2,18},{4,20},{6,22},{8,24},{10,26},{12,28},{14,30},{16,0},... | collective-permute-start | bytes 399368 | tf_op jit(solution)/shard_map/ppermute | solution.py:221
  7.8 46.8 %collective-permute-start.9 = (bf16[1,1,1,1,104,640]{5,4,3,2,1,0:T(8,128)(2,1)S(1)}, bf16[1,1,1,1,104,640]{5,4,3,2,1,0:T(8,128)(2,1)}, u32[]{:S(2)}, u32[]{:S(2)}) collective-permute-start(bf16[1,1,1,1,104,640]{5,4,3,2,1,0:T(8,128)(2,1)S(1)} %get-tuple-element.21), channel_id=1, source_target_pairs={{0,16},{2,18},{4,20},{6,22},{8,24},{10,26},{12,28},{14,30},{16,0},... | collective-permute-start | bytes 399368 | tf_op jit(solution)/shard_map/ppermute | solution.py:221
  8.1 47.9 %collective-permute-start.13 = (bf16[1,1,1,1,104,640]{5,4,3,2,1,0:T(8,128)(2,1)S(1)}, bf16[1,1,1,1,104,640]{5,4,3,2,1,0:T(8,128)(2,1)S(1)}, u32[]{:S(2)}, u32[]{:S(2)}) collective-permute-start(bf16[1,1,1,1,104,640]{5,4,3,2,1,0:T(8,128)(2,1)S(1)} %get-tuple-element.20), channel_id=1, source_target_pairs={{0,4},{2,6},{4,0},{6,2},{8,12},{10,14},{12,8},{14,10},{16,20},{18,... | collective-permute-start | bytes 399368 | tf_op jit(solution)/shard_map/ppermute | solution.py:221
  45.6 71.7 %collective-permute-start.24 = (f32[832,640]{1,0:T(8,128)}, f32[832,640]{1,0:T(8,128)}, u32[]{:S(2)}, u32[]{:S(2)}) collective-permute-start(f32[832,640]{1,0:T(8,128)} %fusion.6), channel_id=1, source_target_pairs={{0,2},{2,0},{4,6},{6,4},{8,10},{10,8},{12,14},{14,12},{16,18},{18,... | collective-permute-start | bytes 6389768 | tf_op jit(solution)/shard_map/ppermute | solution.py:221
  52.9 19.5 %collective-permute-start.6 = (bf16[1,1,1,2,104,640]{5,4,3,2,1,0:T(8,128)(2,1)S(1)}, bf16[1,1,1,2,104,640]{5,4,3,2,1,0:T(8,128)(2,1)S(1)}, u32[]{:S(2)}, u32[]{:S(2)}) collective-permute-start(bf16[1,1,1,2,104,640]{5,4,3,2,1,0:T(8,128)(2,1)S(1)} %pad_maximum_fusion.15), channel_id=1, source_target_pairs={{0,8},{2,10},{4,12},{6,14},{8,0},{10,2},{12,4},{14,6},{16,24},{18,... | collective-permute-start | bytes 798728 | tf_op jit(solution)/shard_map/ppermute | solution.py:221
  55.5 22.7 %collective-permute-start.10 = (bf16[1,1,1,2,104,640]{5,4,3,2,1,0:T(8,128)(2,1)S(1)}, bf16[1,1,1,2,104,640]{5,4,3,2,1,0:T(8,128)(2,1)S(1)}, u32[]{:S(2)}, u32[]{:S(2)}) collective-permute-start(bf16[1,1,1,2,104,640]{5,4,3,2,1,0:T(8,128)(2,1)S(1)} %pad_maximum_fusion.16), channel_id=1, source_target_pairs={{0,8},{2,10},{4,12},{6,14},{8,0},{10,2},{12,4},{14,6},{16,24},{18,... | collective-permute-start | bytes 798728 | tf_op jit(solution)/shard_map/ppermute | solution.py:221
  56.0 23.9 %collective-permute-start.14 = (bf16[1,2,1,1,104,640]{5,4,3,2,1,0:T(8,128)(2,1)S(1)}, bf16[1,2,1,1,104,640]{5,4,3,2,1,0:T(8,128)(2,1)S(1)}, u32[]{:S(2)}, u32[]{:S(2)}) collective-permute-start(bf16[1,2,1,1,104,640]{5,4,3,2,1,0:T(8,128)(2,1)S(1)} %pad_maximum_fusion.17), channel_id=1, source_target_pairs={{0,16},{2,18},{4,20},{6,22},{8,24},{10,26},{12,28},{14,30},{16,0},... | collective-permute-start | bytes 798728 | tf_op jit(solution)/shard_map/ppermute | solution.py:221
  66.0 22.8 %collective-permute-start.2 = (bf16[1,2,1,2,104,640]{5,4,3,2,1,0:T(8,128)(2,1)S(1)}, bf16[1,2,1,2,104,640]{5,4,3,2,1,0:T(8,128)(2,1)S(1)}, u32[]{:S(2)}, u32[]{:S(2)}) collective-permute-start(bf16[1,2,1,2,104,640]{5,4,3,2,1,0:T(8,128)(2,1)S(1)} %pad_maximum_fusion.8), channel_id=1, source_target_pairs={{0,8},{2,10},{4,12},{6,14},{8,0},{10,2},{12,4},{14,6},{16,24},{18,... | collective-permute-start | bytes 1597448 | tf_op jit(solution)/shard_map/ppermute | solution.py:221
  73.4 18.3 %collective-permute-start.7 = (bf16[1,1,2,2,104,640]{5,4,3,2,1,0:T(8,128)(2,1)S(1)}, bf16[1,1,2,2,104,640]{5,4,3,2,1,0:T(8,128)(2,1)}, u32[]{:S(2)}, u32[]{:S(2)}) collective-permute-start(bf16[1,1,2,2,104,640]{5,4,3,2,1,0:T(8,128)(2,1)S(1)} %pad_maximum_fusion.9), channel_id=1, source_target_pairs={{0,4},{2,6},{4,0},{6,2},{8,12},{10,14},{12,8},{14,10},{16,20},{18,... | collective-permute-start | bytes 1597448 | tf_op jit(solution)/shard_map/ppermute | solution.py:221
  78.2 42.4 %collective-permute-start.29 = (f32[832,640]{1,0:T(8,128)}, f32[832,640]{1,0:T(8,128)}, u32[]{:S(2)}, u32[]{:S(2)}) collective-permute-start(f32[832,640]{1,0:T(8,128)} %fusion.3), channel_id=1, source_target_pairs={{0,2},{2,0},{4,6},{6,4},{8,10},{10,8},{12,14},{14,12},{16,18},{18,... | collective-permute-start | bytes 6389768 | tf_op jit(solution)/shard_map/ppermute | solution.py:221
  79.9 26.6 %collective-permute-start.11 = (bf16[1,1,2,2,104,640]{5,4,3,2,1,0:T(8,128)(2,1)}, bf16[1,1,2,2,104,640]{5,4,3,2,1,0:T(8,128)(2,1)S(1)}, u32[]{:S(2)}, u32[]{:S(2)}) collective-permute-start(bf16[1,1,2,2,104,640]{5,4,3,2,1,0:T(8,128)(2,1)} %pad_maximum_fusion.10), channel_id=1, source_target_pairs={{0,4},{2,6},{4,0},{6,2},{8,12},{10,14},{12,8},{14,10},{16,20},{18,... | collective-permute-start | bytes 1597448 | tf_op jit(solution)/shard_map/ppermute | solution.py:221
  91.7 22.0 %collective-permute-start.3 = (bf16[1,2,2,2,104,640]{5,4,3,2,1,0:T(8,128)(2,1)}, bf16[1,2,2,2,104,640]{5,4,3,2,1,0:T(8,128)(2,1)}, u32[]{:S(2)}, u32[]{:S(2)}) collective-permute-start(bf16[1,2,2,2,104,640]{5,4,3,2,1,0:T(8,128)(2,1)} %pad_maximum_fusion.4), channel_id=1, source_target_pairs={{0,2},{2,0},{4,6},{6,4},{8,10},{10,8},{12,14},{14,12},{16,18},{18,... | collective-permute-start | bytes 3194888 | tf_op jit(solution)/shard_map/ppermute | solution.py:221
  106.5 18.6 %collective-permute-start.34 = (f32[832,640]{1,0:T(8,128)}, f32[832,640]{1,0:T(8,128)S(1)}, u32[]{:S(2)}, u32[]{:S(2)}) collective-permute-start(f32[832,640]{1,0:T(8,128)} %fusion), channel_id=1, source_target_pairs={{0,2},{2,0},{4,6},{6,4},{8,10},{10,8},{12,14},{14,12},{16,18},{18,... | collective-permute-start | bytes 6389768 | tf_op jit(solution)/shard_map/ppermute | solution.py:221
  113.8 57.6 %collective-permute-start.18 = (f32[832,640]{1,0:T(8,128)}, f32[832,640]{1,0:T(8,128)S(1)}, u32[]{:S(2)}, u32[]{:S(2)}) collective-permute-start(f32[832,640]{1,0:T(8,128)} %fusion.9), channel_id=1, source_target_pairs={{0,2},{2,0},{4,6},{6,4},{8,10},{10,8},{12,14},{14,12},{16,18},{18,... | collective-permute-start | bytes 6389768 | tf_op jit(solution)/shard_map/ppermute | solution.py:221
  120.6 26.4 %collective-permute-start.25 = (f32[1,1,2,2,104,640]{5,4,3,2,1,0:T(8,128)S(1)}, f32[1,1,2,2,104,640]{5,4,3,2,1,0:T(8,128)S(1)}, u32[]{:S(2)}, u32[]{:S(2)}) collective-permute-start(f32[1,1,2,2,104,640]{5,4,3,2,1,0:T(8,128)S(1)} %slice.114), channel_id=1, source_target_pairs={{0,4},{2,6},{4,0},{6,2},{8,12},{10,14},{12,8},{14,10},{16,20},{18,... | collective-permute-start | bytes 3194888 | tf_op jit(solution)/shard_map/ppermute | solution.py:221
  125.2 43.8 %collective-permute-start.30 = (f32[1,1,2,2,104,640]{5,4,3,2,1,0:T(8,128)S(1)}, f32[1,1,2,2,104,640]{5,4,3,2,1,0:T(8,128)S(1)}, u32[]{:S(2)}, u32[]{:S(2)}) collective-permute-start(f32[1,1,2,2,104,640]{5,4,3,2,1,0:T(8,128)S(1)} %slice.120), channel_id=1, source_target_pairs={{0,4},{2,6},{4,0},{6,2},{8,12},{10,14},{12,8},{14,10},{16,20},{18,... | collective-permute-start | bytes 3194888 | tf_op jit(solution)/shard_map/ppermute | solution.py:221
  127.0 43.3 %collective-permute-start.35 = (f32[1,2,1,2,104,640]{5,4,3,2,1,0:T(8,128)S(1)}, f32[1,2,1,2,104,640]{5,4,3,2,1,0:T(8,128)S(1)}, u32[]{:S(2)}, u32[]{:S(2)}) collective-permute-start(f32[1,2,1,2,104,640]{5,4,3,2,1,0:T(8,128)S(1)} %slice.126), channel_id=1, source_target_pairs={{0,8},{2,10},{4,12},{6,14},{8,0},{10,2},{12,4},{14,6},{16,24},{18,... | collective-permute-start | bytes 3194888 | tf_op jit(solution)/shard_map/ppermute | solution.py:221
  129.5 120.5 %collective-permute-start.17 = (f32[832,640]{1,0:T(8,128)}, f32[832,640]{1,0:T(8,128)S(1)}, u32[]{:S(2)}, u32[]{:S(2)}) collective-permute-start(f32[832,640]{1,0:T(8,128)} %fusion.12), channel_id=1, source_target_pairs={{0,2},{2,0},{4,6},{6,4},{8,10},{10,8},{12,14},{14,12},{16,18},{18,... | collective-permute-start | bytes 6389768 | tf_op jit(solution)/shard_map/ppermute | solution.py:221
  147.0 86.8 %collective-permute-start.4 = (bf16[1664,640]{1,0:T(8,128)(2,1)S(1)}, bf16[1664,640]{1,0:T(8,128)(2,1)S(1)}, u32[]{:S(2)}, u32[]{:S(2)}) collective-permute-start(bf16[1664,640]{1,0:T(8,128)(2,1)S(1)} %bitcast.54), channel_id=1, source_target_pairs={{0,1},{1,0},{2,3},{3,2},{4,5},{5,4},{6,7},{7,6},{8,9},{9,8},{10,11... | collective-permute-start | bytes 6389768 | tf_op jit(solution)/shard_map/ppermute | solution.py:220
  169.0 26.4 %collective-permute-start.26 = (f32[1,1,1,2,104,640]{5,4,3,2,1,0:T(8,128)S(1)}, f32[1,1,1,2,104,640]{5,4,3,2,1,0:T(8,128)S(1)}, u32[]{:S(2)}, u32[]{:S(2)}) collective-permute-start(f32[1,1,1,2,104,640]{5,4,3,2,1,0:T(8,128)S(1)} %slice.116), channel_id=1, source_target_pairs={{0,8},{2,10},{4,12},{6,14},{8,0},{10,2},{12,4},{14,6},{16,24},{18,... | collective-permute-start | bytes 1597448 | tf_op jit(solution)/shard_map/ppermute | solution.py:221
  170.4 34.7 %collective-permute-start.31 = (f32[1,1,1,2,104,640]{5,4,3,2,1,0:T(8,128)S(1)}, f32[1,1,1,2,104,640]{5,4,3,2,1,0:T(8,128)S(1)}, u32[]{:S(2)}, u32[]{:S(2)}) collective-permute-start(f32[1,1,1,2,104,640]{5,4,3,2,1,0:T(8,128)S(1)} %slice.122), channel_id=1, source_target_pairs={{0,8},{2,10},{4,12},{6,14},{8,0},{10,2},{12,4},{14,6},{16,24},{18,... | collective-permute-start | bytes 1597448 | tf_op jit(solution)/shard_map/ppermute | solution.py:221
  171.4 34.4 %collective-permute-start.36 = (f32[1,2,1,1,104,640]{5,4,3,2,1,0:T(8,128)S(1)}, f32[1,2,1,1,104,640]{5,4,3,2,1,0:T(8,128)S(1)}, u32[]{:S(2)}, u32[]{:S(2)}) collective-permute-start(f32[1,2,1,1,104,640]{5,4,3,2,1,0:T(8,128)S(1)} %slice.128), channel_id=1, source_target_pairs={{0,16},{2,18},{4,20},{6,22},{8,24},{10,26},{12,28},{14,30},{16,0},... | collective-permute-start | bytes 1597448 | tf_op jit(solution)/shard_map/ppermute | solution.py:221
  195.4 54.6 %collective-permute-start.19 = (f32[832,640]{1,0:T(8,128)S(1)}, f32[832,640]{1,0:T(8,128)S(1)}, u32[]{:S(2)}, u32[]{:S(2)}) collective-permute-start(f32[832,640]{1,0:T(8,128)S(1)} %convolution_add_fusion.3), channel_id=1, source_target_pairs={{0,1},{1,0},{2,3},{3,2},{4,5},{5,4},{6,7},{7,6},{8,9},{9,8},{10,11... | collective-permute-start | bytes 6389768 | tf_op jit(solution)/shard_map/ppermute | solution.py:220
  205.1 18.9 %collective-permute-start.27 = (f32[1,1,1,1,104,640]{5,4,3,2,1,0:T(8,128)S(1)}, f32[1,1,1,1,104,640]{5,4,3,2,1,0:T(8,128)S(1)}, u32[]{:S(2)}, u32[]{:S(2)}) collective-permute-start(f32[1,1,1,1,104,640]{5,4,3,2,1,0:T(8,128)S(1)} %slice.118), channel_id=1, source_target_pairs={{0,16},{2,18},{4,20},{6,22},{8,24},{10,26},{12,28},{14,30},{16,0},... | collective-permute-start | bytes 798728 | tf_op jit(solution)/shard_map/ppermute | solution.py:221
  205.8 23.9 %collective-permute-start.32 = (f32[1,1,1,1,104,640]{5,4,3,2,1,0:T(8,128)S(1)}, f32[1,1,1,1,104,640]{5,4,3,2,1,0:T(8,128)S(1)}, u32[]{:S(2)}, u32[]{:S(2)}) collective-permute-start(f32[1,1,1,1,104,640]{5,4,3,2,1,0:T(8,128)S(1)} %slice.124), channel_id=1, source_target_pairs={{0,16},{2,18},{4,20},{6,22},{8,24},{10,26},{12,28},{14,30},{16,0},... | collective-permute-start | bytes 798728 | tf_op jit(solution)/shard_map/ppermute | solution.py:221
  229.6 133.0 %collective-permute-start.28 = (f32[104,640]{1,0:T(8,128)S(1)}, f32[104,640]{1,0:T(8,128)}, u32[]{:S(2)}, u32[]{:S(2)}) collective-permute-start(f32[104,640]{1,0:T(8,128)S(1)} %fusion.20), channel_id=1, source_target_pairs={{0,1},{1,0},{2,3},{3,2},{4,5},{5,4},{6,7},{7,6},{8,9},{9,8},{10,11... | collective-permute-start | bytes 798728 | tf_op jit(solution)/shard_map/ppermute | solution.py:220
  232.2 131.4 %collective-permute-start.33 = (f32[104,640]{1,0:T(8,128)S(1)}, f32[104,640]{1,0:T(8,128)}, u32[]{:S(2)}, u32[]{:S(2)}) collective-permute-start(f32[104,640]{1,0:T(8,128)S(1)} %fusion.19), channel_id=1, source_target_pairs={{0,1},{1,0},{2,3},{3,2},{4,5},{5,4},{6,7},{7,6},{8,9},{9,8},{10,11... | collective-permute-start | bytes 798728 | tf_op jit(solution)/shard_map/ppermute | solution.py:220
  233.8 130.8 %collective-permute-start.38 = (f32[104,640]{1,0:T(8,128)S(1)}, f32[104,640]{1,0:T(8,128)}, u32[]{:S(2)}, u32[]{:S(2)}) collective-permute-start(f32[104,640]{1,0:T(8,128)S(1)} %fusion.18), channel_id=1, source_target_pairs={{0,1},{1,0},{2,3},{3,2},{4,5},{5,4},{6,7},{7,6},{8,9},{9,8},{10,11... | collective-permute-start | bytes 798728 | tf_op jit(solution)/shard_map/ppermute | solution.py:220
  250.5 24.0 %collective-permute-start.20 = (f32[1,2,1,2,104,640]{5,4,3,2,1,0:T(8,128)S(1)}, f32[1,2,1,2,104,640]{5,4,3,2,1,0:T(8,128)S(1)}, u32[]{:S(2)}, u32[]{:S(2)}) collective-permute-start(f32[1,2,1,2,104,640]{5,4,3,2,1,0:T(8,128)S(1)} %slice.108), channel_id=1, source_target_pairs={{0,8},{2,10},{4,12},{6,14},{8,0},{10,2},{12,4},{14,6},{16,24},{18,... | collective-permute-start | bytes 3194888 | tf_op jit(solution)/shard_map/ppermute | solution.py:221
  274.6 24.0 %collective-permute-start.21 = (f32[1,2,1,1,104,640]{5,4,3,2,1,0:T(8,128)S(1)}, f32[1,2,1,1,104,640]{5,4,3,2,1,0:T(8,128)S(1)}, u32[]{:S(2)}, u32[]{:S(2)}) collective-permute-start(f32[1,2,1,1,104,640]{5,4,3,2,1,0:T(8,128)S(1)} %slice.110), channel_id=1, source_target_pairs={{0,16},{2,18},{4,20},{6,22},{8,24},{10,26},{12,28},{14,30},{16,0},... | collective-permute-start | bytes 1597448 | tf_op jit(solution)/shard_map/ppermute | solution.py:221
  307.1 55.4 %collective-permute-start.23 = (f32[104,640]{1,0:T(8,128)S(1)}, f32[104,640]{1,0:T(8,128)S(1)}, u32[]{:S(2)}, u32[]{:S(2)}) collective-permute-start(f32[104,640]{1,0:T(8,128)S(1)} %fusion.21), channel_id=1, source_target_pairs={{0,1},{1,0},{2,3},{3,2},{4,5},{5,4},{6,7},{7,6},{8,9},{9,8},{10,11... | collective-permute-start | bytes 798728 | tf_op jit(solution)/shard_map/ppermute | solution.py:220
  (23 other events, 248.2 us)

commit v2 on v1

--- a/solution.py
+++ b/solution.py
@@ -169,24 +169,37 @@
     )(clip_counts, projected, projected, projected, cosine, sine)
 
 
-def attention_backward(projected, clip_counts, grad_t, cosine, sine):
+def attention_backward(projected, clip_counts, grad_t, cosine, sine, heads_from, heads_to, before):
     rows = projected.shape[0]
     heads = projected.shape[1] // 3 // HS
+    count = heads_to - heads_from
     whole = pl.BlockSpec((rows, HS), lambda h, j, c: (0, 0))
+    at = heads_from
+    in_specs = [
+        pl.BlockSpec((rows, HS), lambda h, j, c: (0, at + h)),
+        pl.BlockSpec((rows, HS), lambda h, j, c: (0, at + h + heads)),
+        pl.BlockSpec((rows, HS), lambda h, j, c: (0, at + h + 2 * heads)),
+        pl.BlockSpec((HS, rows), lambda h, j, c: (at + h, 0)),
+        whole,
+        whole,
+    ]
+    operands = [clip_counts, projected, projected, projected, grad_t, cosine, sine]
+    kernel, aliases = backward_kernel, {}
+    if before is not None:
+        in_specs.append(pl.BlockSpec(memory_space=pl.ANY))
+        aliases = {len(operands): 0}
+        operands.append(before)
+
+        def kernel(*refs):
+            backward_kernel(*refs[:7], *refs[8:])
+
     return pl.pallas_call(
-        backward_kernel,
+        kernel,
         grid_spec=pltpu.PrefetchScalarGridSpec(
             num_scalar_prefetch=1,
-            grid=(heads, 3),
-            in_specs=[
-                pl.BlockSpec((rows, HS), lambda h, j, c: (0, h)),
-                pl.BlockSpec((rows, HS), lambda h, j, c: (0, h + heads)),
-                pl.BlockSpec((rows, HS), lambda h, j, c: (0, h + 2 * heads)),
-                pl.BlockSpec((HS, rows), lambda h, j, c: (h, 0)),
-                whole,
-                whole,
-            ],
-            out_specs=pl.BlockSpec((rows, HS), lambda h, j, c: (0, j * heads + h)),
+            grid=(count, 3),
+            in_specs=in_specs,
+            out_specs=pl.BlockSpec((rows, HS), lambda h, j, c: (0, j * heads + at + h)),
             scratch_shapes=[
                 pltpu.VMEM((rows, HS), jnp.bfloat16),
                 pltpu.VMEM((rows, HS), jnp.bfloat16),
@@ -196,12 +209,13 @@
             ],
         ),
         out_shape=jax.ShapeDtypeStruct(projected.shape, jnp.bfloat16),
+        input_output_aliases=aliases,
         compiler_params=pltpu.CompilerParams(vmem_limit_bytes=VMEM_BYTES),
         cost_estimate=pl.CostEstimate(
-            flops=heads * rows * rows * HS * 14, bytes_accessed=rows * heads * HS * 14,
-            transcendentals=heads * rows * rows,
+            flops=count * rows * rows * HS * 70, bytes_accessed=rows * count * HS * 14,
+            transcendentals=count * rows * rows,
         ),
-    )(clip_counts, projected, projected, projected, grad_t, cosine, sine)
+    )(*operands)
 
 
 def body(sizes, projected, cotangent, out_weight, clip_counts, tube_index):
@@ -209,6 +223,7 @@
     bits = devices.bit_length() - 1
     rows = projected.shape[0]
     head_width = projected.shape[1] // 3
+    heads = head_width // HS
     depth = out_weight.shape[0]
     width = out_weight.shape[1]
     piece = width // CHUNKS
@@ -220,99 +235,146 @@
             return lax.ppermute(array, "dp", [(i, i ^ 1) for i in range(pair)])
         return lax.ppermute(array, "fsdp", [(i, i ^ (1 << bit)) for i in range(devices)])
 
-    slot = np.array([int(format(i, f"0{bits}b")[::-1], 2) for i in range(devices)])
+    slot_of = [int(format(i, f"0{bits}b")[::-1], 2) for i in range(devices)]
 
     def to_places(array):
         return jnp.concatenate(
-            [
-                lax.dynamic_slice_in_dim(array, (int(p) ^ me) * depth, depth, 0)
-                for p in slot
-            ],
+            [lax.dynamic_slice_in_dim(array, (p ^ me) * depth, depth, 0) for p in slot_of],
             axis=0,
         )
 
-    def from_places(array):
-        table = jnp.asarray(slot, dtype=jnp.int32)
-        return jnp.concatenate(
-            [
-                lax.dynamic_slice_in_dim(array, table[j ^ me] * depth, depth, 0)
-                for j in range(devices)
-            ],
-            axis=0,
-        )
-
-    x_bit, z_bits = 1, list(range(2, bits))
-
-    def gather(part, order):
-        array = part.reshape((1,) * bits + part.shape)
-        for bit in order:
-            array = jnp.concatenate([array, across(array, bit)], axis=bit)
-        return array.reshape(devices * depth, piece)
-
-    def reduce(keep, send, order):
-        array = keep + across(send, 0)
-        array = array.reshape((1,) + (2,) * (bits - 1) + (depth, piece))
-        for bit in order:
-            if bit < 0:
-                continue
-            send = lax.slice_in_dim(array, 1, 2, axis=bit)
-            keep = lax.slice_in_dim(array, 0, 1, axis=bit)
-            array = keep + across(send, bit)
-        return array.reshape(depth, piece)
-
-    weight_copy = out_weight.astype(jnp.bfloat16)
-
-    def columns(array, index):
-        return lax.dynamic_slice_in_dim(array, index * piece, piece, 1)
-
-    down = z_bits[::-1]
-    own = gather(columns(weight_copy, row_side), [x_bit] + down + [0])
-    other = across(own, -1)
-    weights = [jnp.where(row_side == 0, own, other), jnp.where(row_side == 0, other, own)]
-    for index in (2, 3):
-        weights.append(gather(columns(weight_copy, index), down + [x_bit, 0]))
-    weights.append(gather(columns(weight_copy, 4), [x_bit] + down + [0]))
-    full_weight = jnp.concatenate(weights, axis=1)
-
+    def part_of(array, bit, which):
+        return lax.slice_in_dim(array, which, which + 1, axis=bit)
+
+    def together(sends, work_in, work):
+        arrays, work_in = lax.optimization_barrier(([a for a, _ in sends], work_in))
+        arrived = [across(a, bit) for a, (_, bit) in zip(arrays, sends)]
+        return lax.optimization_barrier((arrived, work(work_in)))
+
+    full_weight = lax.all_gather(out_weight.astype(jnp.bfloat16), "fsdp", axis=0, tiled=True)
     bounds = jnp.cumsum(clip_counts)
     live_rows = (jnp.arange(rows) < bounds[-1]).astype(jnp.bfloat16)[:, None]
     cosine, sine = angles(tube_index)
     masked_cot = cotangent * live_rows
-    attn_t = to_places(attention_forward(projected, clip_counts, cosine, sine))
+    attn_t = attention_forward(projected, clip_counts, cosine, sine)
+    placed_t = to_places(attn_t)
     half = head_width // 2
-    keep_t, send_t = attn_t[:half], attn_t[half:]
+    keep_t, send_t = placed_t[:half], placed_t[half:]
+    cubes = (1,) + (2,) * (bits - 1) + (depth, piece)
 
     def product(left, index):
-        return jnp.dot(left, columns(masked_cot, index), preferred_element_type=jnp.float32)
-
-    mine, theirs = row_side, 1 - row_side
-    own_keep, own_send = product(keep_t, mine), product(send_t, mine)
-    other_keep, other_send = product(keep_t, theirs), product(send_t, theirs)
-    pair_send = other_keep + across(other_send, 0)
-    pair_keep = own_keep + across(own_send, 0)
-    array = pair_keep + across(pair_send, -1)
-    array = array.reshape((1,) + (2,) * (bits - 1) + (depth, piece))
-    for bit in z_bits + [x_bit]:
-        array = lax.slice_in_dim(array, 0, 1, axis=bit) + across(
-            lax.slice_in_dim(array, 1, 2, axis=bit), bit
+        cot = lax.dynamic_slice_in_dim(masked_cot, index * piece, piece, 1)
+        return jnp.dot(left, cot, preferred_element_type=jnp.float32)
+
+    def first_sum(index):
+        sent = across(product(send_t, index), 0)
+        return (product(keep_t, index) + sent).reshape(cubes)
+
+    x, near, far = 1, 2, list(range(3, bits))
+    last = far[-1] if far else None
+    give = first_sum(1 - row_side)
+    second = first_sum(2)
+    fifth = first_sum(4)
+    own = first_sum(row_side)
+    third = first_sum(3)
+
+    def nothing(value):
+        return value
+
+    def step(array, bit):
+        return part_of(array, bit, 0), part_of(array, bit, 1)
+
+    def middle(array):
+        for bit in far[:-1]:
+            low, high = step(array, bit)
+            array = low + across(high, bit)
+        return array
+
+    (g_in, s_in, f_in), _ = together(
+        [(part_of(give, near, 1), -1), (part_of(second, x, 1), x), (part_of(fifth, near, 1), near)],
+        (),
+        nothing,
+    )
+    ahead = part_of(own, near, 1) + g_in
+    second = part_of(second, x, 0) + s_in
+    fifth = middle(part_of(fifth, near, 0) + f_in)
+    (g_in, a_in, t_in, f_in), _ = together(
+        [
+            (part_of(give, near, 0), -1),
+            (ahead, near),
+            (part_of(third, x, 1), x),
+            (part_of(fifth, last, 1), last),
+        ],
+        (),
+        nothing,
+    )
+    own = middle(part_of(own, near, 0) + g_in + a_in)
+    third = part_of(third, x, 0) + t_in
+    fifth = part_of(fifth, last, 0) + f_in
+
+    def grad_of(weight):
+        return lax.dot_general(
+            weight, masked_cot, (((1,), (1,)), ((), ())), preferred_element_type=jnp.float32
+        ).astype(jnp.bfloat16)
+
+    cuts = (0, heads * 2 // 13, heads * 8 // 13, heads)
+
+    def backward(grad_t, index, before):
+        return attention_backward(
+            projected, clip_counts, grad_t, cosine, sine, cuts[index], cuts[index + 1], before
         )
-    own = array.reshape(depth, piece)
-    other = across(own, -1)
-    grads = [jnp.where(row_side == 0, own, other), jnp.where(row_side == 0, other, own)]
-    for index, order in ((2, [x_bit] + z_bits), (3, [x_bit] + z_bits), (4, z_bits + [x_bit])):
-        own = reduce(product(keep_t, index), product(send_t, index), order)
-        grads.append(own + across(own, -1))
-    grad_weight = jnp.concatenate(grads, axis=1)
-
-    grad_t = lax.dot_general(
-        full_weight, masked_cot, (((1,), (1,)), ((), ())), preferred_element_type=jnp.float32
-    ).astype(jnp.bfloat16)
-    grad_projected = attention_backward(
-        projected, clip_counts, from_places(grad_t), cosine, sine
-    )
-    work_out = lax.dot_general(
-        attn_t, full_weight, (((0,), (0,)), ((), ())), preferred_element_type=jnp.float32
-    ).astype(jnp.bfloat16)
+
+    def work_one(weight):
+        grad_t = grad_of(weight)
+        return grad_t, backward(grad_t, 0, None)
+
+    (o_in, s_in, t_in, f_in), (grad_t, grad_projected) = together(
+        [
+            (part_of(own, last, 1), last),
+            (part_of(second, near, 1), near),
+            (part_of(third, near, 1), near),
+            (part_of(fifth, x, 1), x),
+        ],
+        full_weight,
+        work_one,
+    )
+    own = part_of(own, last, 0) + o_in
+    second = middle(part_of(second, near, 0) + s_in)
+    third = middle(part_of(third, near, 0) + t_in)
+    fifth = part_of(fifth, x, 0) + f_in
+    (o_in, s_in, t_in, f_in), (grad_t, grad_projected) = together(
+        [
+            (part_of(own, x, 1), x),
+            (part_of(second, last, 1), last),
+            (part_of(third, last, 1), last),
+            (fifth, -1),
+        ],
+        (grad_t, grad_projected),
+        lambda held: (held[0], backward(held[0], 1, held[1])),
+    )
+    own = part_of(own, x, 0) + o_in
+    second = part_of(second, last, 0) + s_in
+    third = part_of(third, last, 0) + t_in
+    fifth = fifth + f_in
+
+    def work_last(held):
+        grad_t, grad_projected = held
+        out = lax.dot_general(
+            attn_t, full_weight, (((0,), (0,)), ((), ())), preferred_element_type=jnp.float32
+        ).astype(jnp.bfloat16)
+        return out, backward(grad_t, 2, grad_projected)
+
+    (o_in, s_in, t_in), (work_out, grad_projected) = together(
+        [(own, -1), (second, -1), (third, -1)], (grad_t, grad_projected), work_last
+    )
+    pieces = [
+        jnp.where(row_side == 0, own, o_in),
+        jnp.where(row_side == 0, o_in, own),
+        second + s_in,
+        third + t_in,
+        fifth,
+    ]
+    grad_weight = jnp.concatenate([p.reshape(depth, piece) for p in pieces], axis=1)
     return (work_out, grad_projected, grad_weight)
 
 

time: 368 us -> 285 us (0.77)
  waiting for transfers between devices: 149 us -> 84.4 us
  starting transfers between devices: 40.1 us -> 24.2 us
  other arithmetic: 27.4 us -> 14.5 us
  matrix products: 44.9 us -> 52.7 us
    ppermute x33 -> x17, waiting for transfers between devices: 149 us -> 70.6 us  [across(): lax.ppermute(array, 'fsdp', [(i, i ^ 1 << bit) for i in range(devices)])]
    concatenate x17 -> x1, other arithmetic: 17.2 us -> 0.04 us  [body(): jnp.concatenate([p.reshape(depth, piece) for p in pieces], axis=1)]
    ppermute x33 -> x17, starting transfers between devices: 31.7 us -> 16.1 us  [across(): lax.ppermute(array, 'fsdp', [(i, i ^ 1 << bit) for i in range(devices)])]
    ppermute x6, waiting for transfers between devices: 0.02 us -> 13.8 us  [across(): return lax.ppermute(array, 'dp', [(i, i ^ 1) for i in range(pair)])]
    dot_general x12, matrix products: 44.9 us -> 52.7 us  [the longest x10 30.3 us: product(): return jnp.dot(left, cot, preferred_element_type=jnp.float32)]
    add x9 -> x13, other arithmetic: 0.96 us -> 7.68 us  [the longest x1 1.75 us: body(): second = part_of(second, x, 0) + s_in]
    unnamed x70 -> x67, local copies, waits for them, and re-layouts: 18.7 us -> 12 us
    slice x12, local copies, waits for them, and re-layouts: 0.51 us -> 5.75 us  [part_of(): return lax.slice_in_dim(array, which, which + 1, axis=bit)]
  transfers between devices with their start and end apart: 39 -> 24, of which waited for: 14 -> 8; matrix products, arithmetic and copies ran while one was open for 23% -> 22% of each run, Pallas kernels for 20% -> 26%
where the time goes in v2:
time: 285 us; the launch traced here: 284 us
  waiting for transfers between devices  84.4 us (30%)
  Pallas kernels  74.9 us (26%)
  matrix products  52.7 us (18%)
  starting transfers between devices  24.2 us (8%)
  local copies, waits for them, and re-layouts  18.5 us (6%)
  between operations  14.6 us (5%)
  other arithmetic  14.5 us (5%)
    ppermute x17, waiting for transfers between devices, across(): lax.ppermute(array, 'fsdp', [(i, i ^ 1 << bit) for i in range(devices)])  70.6 us
    pallas_call x3, Pallas kernels, attention_backward(): pl.pallas_call(kernel, grid_spec=pltpu.PrefetchScalarGridSpec(num_scalar_...  56.2 us
    dot_general x10, matrix products, product(): return jnp.dot(left, cot, preferred_element_type=jnp.float32)  30.3 us
    pallas_call x1, Pallas kernels, attention_forward(): pl.pallas_call(forward_kernel, grid_spec=pltpu.PrefetchScalarGridSpec(num...  18.7 us
    ppermute x17, starting transfers between devices, across(): lax.ppermute(array, 'fsdp', [(i, i ^ 1 << bit) for i in range(devices)])  16.1 us
    ppermute x6, waiting for transfers between devices, across(): return lax.ppermute(array, 'dp', [(i, i ^ 1) for i in range(pair)])  13.8 us
    dot_general x1, matrix products, grad_of(): lax.dot_general(weight, masked_cot, (((1,), (1,)), ((), ())), preferred_e...  12.8 us
    unnamed x67, local copies, waits for them, and re-layouts  12 us
  transfers between devices with their start and end apart: 24, of which 8 were waited for; matrix products, arithmetic and copies ran while one was open for 22% of the time, Pallas kernels for 26%

profile of v2, /device:TPU:0, one launch (start us, length us, event | category | flops | bytes accessed | tf_op | source)
XLA Modules:
  0.0 283.9 jit_solution(12006590672260081001)
XLA Ops:
  7.3 2.3 convert_element_type.29
  11.0 2.4 fusion.18
  13.7 18.7 %shard_map.94 = bf16[1664,640]{1,0:T(8,128)(2,1)S(1)} custom-call(s32[2]{0:T(128)S(1)} %copy-done, bf16[640,4992]{1,0:T(8,128)(2,1)} %refs_3_.3, bf16[640,4992]{1,0:T(8,128)(2,1)} %refs_3_.3, bf16[640,4992]{1,0:T(8,128)(2,1)} %refs_3_.3, f32[640,128]{1,0:T(8,128)S(1)} %get-tuple-element.121.cos_ref.refs_5_, f32[640,128]{1,0:T(8,128)S(1)} %get-tuple-element.122.sin_ref.refs_6_), custom_call_target="tpu_custom_call" | custom-call | flops 4089446400 | bytes 8519680 | tf_op jit(solution)/shard_map/pallas_call | solution.py:144
  38.3 2.7 fusion.4
  41.4 2.4 fusion.7
  43.9 4.0 %fusion.10 = f32[832,640]{1,0:T(8,128)} fusion(bf16[832,640]{1,0:T(8,128)(2,1)} %copy-done.23, bf16[640,3200]{1,0:T(8,128)(2,1)} %copy-done.3, s32[]{:T(128)S(6)} %select_n.118), kind=kOutput, calls=%fused_computation.23 | convolution fusion | flops 681574400 | bytes 4014084 | tf_op jit(solution)/shard_map/dot_general | solution.py:267
  48.3 3.7 %fusion.1 = f32[832,640]{1,0:T(8,128)} fusion(bf16[832,640]{1,0:T(8,128)(2,1)S(1)} %copy-done.24, bf16[640,3200]{1,0:T(8,128)(2,1)} %copy-done.3), kind=kOutput, calls=%fused_computation.14 | convolution fusion | flops 681574400 | bytes 4014080 | tf_op jit(solution)/shard_map/dot_general | solution.py:267
  52.1 3.0 %fusion.13 = f32[832,640]{1,0:T(8,128)S(1)} fusion(bf16[832,640]{1,0:T(8,128)(2,1)} %copy-done.23, bf16[640,3200]{1,0:T(8,128)(2,1)} %copy-done.3, s32[]{:T(128)S(6)} %select_n.109), kind=kOutput, calls=%fused_computation.26 | convolution fusion | flops 681574400 | bytes 4014084 | tf_op jit(solution)/shard_map/dot_general | solution.py:267
  55.4 3.0 %convolution_add_fusion.1 = f32[832,640]{1,0:T(8,128)S(1)} fusion(f32[832,640]{1,0:T(8,128)} %collective-permute-done.3, bf16[832,640]{1,0:T(8,128)(2,1)} %get-tuple-element.99, bf16[640,3200]{1,0:T(8,128)(2,1)S(1)} %copy-done.4), kind=kOutput, calls=%fused_computation.4 | convolution fusion | flops 682106880 | bytes 6144000 | tf_op jit(solution)/shard_map/dot_general | solution.py:267
  58.5 3.1 %convolution_add_fusion.2 = f32[832,640]{1,0:T(8,128)S(1)} fusion(f32[832,640]{1,0:T(8,128)} %collective-permute-done.2, bf16[832,640]{1,0:T(8,128)(2,1)} %get-tuple-element.99, bf16[640,3200]{1,0:T(8,128)(2,1)S(1)} %copy-done.4), kind=kOutput, calls=%fused_computation.5 | convolution fusion | flops 682106880 | bytes 6144000 | tf_op jit(solution)/shard_map/dot_general | solution.py:267
  62.9 3.0 %convolution_add_fusion.3 = f32[832,640]{1,0:T(8,128)S(1)} fusion(f32[832,640]{1,0:T(8,128)} %collective-permute-done.1, bf16[832,640]{1,0:T(8,128)(2,1)} %get-tuple-element.99, bf16[640,3200]{1,0:T(8,128)(2,1)S(1)} %copy-done.4, s32[]{:T(128)S(6)} %select_n.118), kind=kOutput, calls=%fused_computation.6 | convolution fusion | flops 682106880 | bytes 6144004 | tf_op jit(solution)/shard_map/dot_general | solution.py:267
  67.1 2.5 collective-permute-start.4
  72.8 3.0 %convolution_add_fusion = f32[832,640]{1,0:T(8,128)S(1)} fusion(f32[832,640]{1,0:T(8,128)} %collective-permute-done.7, bf16[832,640]{1,0:T(8,128)(2,1)} %get-tuple-element.99, bf16[640,3200]{1,0:T(8,128)(2,1)S(1)} %copy-done.4), kind=kOutput, calls=%fused_computation.3 | convolution fusion | flops 682106880 | bytes 6144000 | tf_op jit(solution)/shard_map/dot_general | solution.py:267
  77.6 2.3 convolution_add_fusion.4
  79.9 13.8 %collective-permute-done.4 = f32[1,2,1,2,104,640]{5,4,3,2,1,0:T(8,128)S(1)} collective-permute-done((f32[1,2,1,2,104,640]{5,4,3,2,1,0:T(8,128)S(1)}, f32[1,2,1,2,104,640]{5,4,3,2,1,0:T(8,128)S(1)}, u32[]{:S(2)}, u32[]{:S(2)}) %collective-permute-start.4) | collective-permute-done | bytes 1064992 | tf_op jit(solution)/shard_map/ppermute | solution.py:235
  93.7 11.0 %collective-permute-done.5 = f32[1,1,2,2,104,640]{5,4,3,2,1,0:T(8,128)S(1)} collective-permute-done((f32[1,1,2,2,104,640]{5,4,3,2,1,0:T(8,128)S(1)}, f32[1,1,2,2,104,640]{5,4,3,2,1,0:T(8,128)S(1)}, u32[]{:S(2)}, u32[]{:S(2)}) %collective-permute-start.5) | collective-permute-done | bytes 1064992 | tf_op jit(solution)/shard_map/ppermute | solution.py:236
  104.7 14.3 %collective-permute-done.6 = f32[1,2,1,2,104,640]{5,4,3,2,1,0:T(8,128)S(1)} collective-permute-done((f32[1,2,1,2,104,640]{5,4,3,2,1,0:T(8,128)S(1)}, f32[1,2,1,2,104,640]{5,4,3,2,1,0:T(8,128)S(1)}, u32[]{:S(2)}, u32[]{:S(2)}) %collective-permute-start.6) | collective-permute-done | bytes 1064992 | tf_op jit(solution)/shard_map/ppermute | solution.py:236
  123.4 2.9 %collective-permute-start.11 = (f32[1,2,1,1,104,640]{5,4,3,2,1,0:T(8,128)S(1)}, f32[1,2,1,1,104,640]{5,4,3,2,1,0:T(8,128)}, u32[]{:S(2)}, u32[]{:S(2)}) collective-permute-start(f32[1,2,1,1,104,640]{5,4,3,2,1,0:T(8,128)S(1)} %slice.123), channel_id=1, source_target_pairs={{0,16},{2,18},{4,20},{6,22},{8,24},{10,26},{12,28},{14,30},{16,0},... | collective-permute-start | bytes 1597448 | tf_op jit(solution)/shard_map/ppermute | solution.py:236
  126.3 1.7 slice_add_fusion.1
  128.9 28.8 %collective-permute-done.11 = f32[1,2,1,1,104,640]{5,4,3,2,1,0:T(8,128)} collective-permute-done((f32[1,2,1,1,104,640]{5,4,3,2,1,0:T(8,128)S(1)}, f32[1,2,1,1,104,640]{5,4,3,2,1,0:T(8,128)}, u32[]{:S(2)}, u32[]{:S(2)}) %collective-permute-start.11) | collective-permute-done | bytes 532512 | tf_op jit(solution)/shard_map/ppermute | solution.py:236
  157.7 2.3 collective-permute-done.9
  165.2 1.7 fusion
  168.7 12.8 %convolution_convert_fusion.1.g_ref.refs_4_ = bf16[1664,640]{1,0:T(8,128)(2,1)S(1)} fusion(bf16[1664,3200]{1,0:T(8,128)(2,1)} %all-gather.2.cloned.1.call-done, bf16[640,3200]{1,0:T(8,128)(2,1)} %copy-done.3), kind=kOutput, calls=%fused_computation.1 | convolution fusion | flops 6816808960 | bytes 16875520 | tf_op jit(solution)/shard_map/dot_general | solution.py:316
  182.8 1.7 collective-permute-start.13
  185.4 9.7 %convolution_convert_fusion = bf16[640,3200]{1,0:T(8,128)(2,1)} fusion(bf16[1664,640]{1,0:T(8,128)(2,1)S(1)} %shard_map.94, bf16[1664,3200]{1,0:T(8,128)(2,1)S(1)} %copy-done.29), kind=kOutput, calls=%fused_computation | convolution fusion | flops 6817792000 | bytes 16875520 | tf_op jit(solution)/shard_map/dot_general | solution.py:362
  195.0 9.3 %shard_map.95.refs_7_ = bf16[640,4992]{1,0:T(8,128)(2,1)} custom-call(s32[2]{0:T(128)S(1)} %copy-done, bf16[640,4992]{1,0:T(8,128)(2,1)} %refs_3_.3, bf16[640,4992]{1,0:T(8,128)(2,1)} %refs_3_.3, bf16[640,4992]{1,0:T(8,128)(2,1)} %refs_3_.3, bf16[1664,640]{1,0:T(8,128)(2,1)S(1)} %convolution_convert_fusion.1.g_ref.refs_4_, ...), custom_call_target="tpu_custom_call" | custom-call | flops 7340032000 | bytes 2293760 | tf_op jit(solution)/shard_map/pallas_call | solution.py:196
  204.3 3.0 %collective-permute-done.12 = f32[1,2,1,1,104,640]{5,4,3,2,1,0:T(8,128)S(1)} collective-permute-done((f32[1,2,1,1,104,640]{5,4,3,2,1,0:T(8,128)S(1)}, f32[1,2,1,1,104,640]{5,4,3,2,1,0:T(8,128)S(1)}, u32[]{:S(2)}, u32[]{:S(2)}) %collective-permute-start.12) | collective-permute-done | bytes 532512 | tf_op jit(solution)/shard_map/ppermute | solution.py:236
  207.3 1.7 collective-permute-done.13
  209.0 9.6 %collective-permute-done.14 = f32[1,1,1,2,104,640]{5,4,3,2,1,0:T(8,128)S(1)} collective-permute-done((f32[1,1,1,2,104,640]{5,4,3,2,1,0:T(8,128)S(1)}, f32[1,1,1,2,104,640]{5,4,3,2,1,0:T(8,128)S(1)}, u32[]{:S(2)}, u32[]{:S(2)}) %collective-permute-start.14) | collective-permute-done | bytes 532512 | tf_op jit(solution)/shard_map/ppermute | solution.py:236
  222.8 1.8 collective-permute-start.18
  225.1 25.5 %shard_map.96.refs_7_ = bf16[640,4992]{1,0:T(8,128)(2,1)} custom-call(s32[2]{0:T(128)S(1)} %copy-done, bf16[640,4992]{1,0:T(8,128)(2,1)} %refs_3_.3, bf16[640,4992]{1,0:T(8,128)(2,1)} %refs_3_.3, bf16[640,4992]{1,0:T(8,128)(2,1)} %refs_3_.3, bf16[1664,640]{1,0:T(8,128)(2,1)S(1)} %convolution_convert_fusion.1.g_ref.refs_4_, ...), custom_call_target="tpu_custom_call", output_to_operand_aliasing={{}: (7, {})} | custom-call | flops 22020096000 | bytes 6881280 | tf_op jit(solution)/shard_map/pallas_call | solution.py:196
  254.3 21.4 %shard_map.97 = bf16[640,4992]{1,0:T(8,128)(2,1)} custom-call(s32[2]{0:T(128)S(1)} %copy-done, bf16[640,4992]{1,0:T(8,128)(2,1)} %refs_3_.3, bf16[640,4992]{1,0:T(8,128)(2,1)} %refs_3_.3, bf16[640,4992]{1,0:T(8,128)(2,1)} %refs_3_.3, bf16[1664,640]{1,0:T(8,128)(2,1)S(1)} %convolution_convert_fusion.1.g_ref.refs_4_, ...), custom_call_target="tpu_custom_call", output_to_operand_aliasing={{}: (7, {})} | custom-call | flops 18350080000 | bytes 5734400 | tf_op jit(solution)/shard_map/pallas_call | solution.py:196
  (138 shorter events, 40.3 us)
Async XLA Ops:
  7.2 161.5 %all-gather.2.cloned.1.call-start = ((), (), s32[]{:S(2)}) async-start(), calls=%async_computation | async-start | bytes 11315200 | tf_op jit(solution)/shard_map/all_gather | solution.py:254
  41.0 14.4 %collective-permute-start.3 = (f32[832,640]{1,0:T(8,128)}, f32[832,640]{1,0:T(8,128)}, u32[]{:S(2)}, u32[]{:S(2)}) collective-permute-start(f32[832,640]{1,0:T(8,128)} %fusion.4), channel_id=1, source_target_pairs={{0,2},{2,0},{4,6},{6,4},{8,10},{10,8},{12,14},{14,12},{16,18},{18,... | collective-permute-start | bytes 6389768 | tf_op jit(solution)/shard_map/ppermute | solution.py:236
  43.8 14.6 %collective-permute-start.2 = (f32[832,640]{1,0:T(8,128)}, f32[832,640]{1,0:T(8,128)}, u32[]{:S(2)}, u32[]{:S(2)}) collective-permute-start(f32[832,640]{1,0:T(8,128)} %fusion.7), channel_id=1, source_target_pairs={{0,2},{2,0},{4,6},{6,4},{8,10},{10,8},{12,14},{14,12},{16,18},{18,... | collective-permute-start | bytes 6389768 | tf_op jit(solution)/shard_map/ppermute | solution.py:236
  47.9 15.0 %collective-permute-start.1 = (f32[832,640]{1,0:T(8,128)}, f32[832,640]{1,0:T(8,128)}, u32[]{:S(2)}, u32[]{:S(2)}) collective-permute-start(f32[832,640]{1,0:T(8,128)} %fusion.10), channel_id=1, source_target_pairs={{0,2},{2,0},{4,6},{6,4},{8,10},{10,8},{12,14},{14,12},{16,18},{18,... | collective-permute-start | bytes 6389768 | tf_op jit(solution)/shard_map/ppermute | solution.py:236
  52.0 20.7 %collective-permute-start.7 = (f32[832,640]{1,0:T(8,128)}, f32[832,640]{1,0:T(8,128)}, u32[]{:S(2)}, u32[]{:S(2)}) collective-permute-start(f32[832,640]{1,0:T(8,128)} %fusion.1), channel_id=1, source_target_pairs={{0,2},{2,0},{4,6},{6,4},{8,10},{10,8},{12,14},{14,12},{16,18},{18,... | collective-permute-start | bytes 6389768 | tf_op jit(solution)/shard_map/ppermute | solution.py:236
  55.1 22.4 %collective-permute-start = (f32[832,640]{1,0:T(8,128)S(1)}, f32[832,640]{1,0:T(8,128)S(1)}, u32[]{:S(2)}, u32[]{:S(2)}) collective-permute-start(f32[832,640]{1,0:T(8,128)S(1)} %fusion.13), channel_id=1, source_target_pairs={{0,2},{2,0},{4,6},{6,4},{8,10},{10,8},{12,14},{14,12},{16,18},{18,... | collective-permute-start | bytes 6389768 | tf_op jit(solution)/shard_map/ppermute | solution.py:236
  67.1 26.6 %collective-permute-start.4 = (f32[1,2,1,2,104,640]{5,4,3,2,1,0:T(8,128)S(1)}, f32[1,2,1,2,104,640]{5,4,3,2,1,0:T(8,128)S(1)}, u32[]{:S(2)}, u32[]{:S(2)}) collective-permute-start(f32[1,2,1,2,104,640]{5,4,3,2,1,0:T(8,128)S(1)} %get-tuple-element.50), channel_id=1, source_target_pairs={{0,1},{1,0},{2,3},{3,2},{4,5},{5,4},{6,7},{7,6},{8,9},{9,8},{10,11... | collective-permute-start | bytes 3194888 | tf_op jit(solution)/shard_map/ppermute | solution.py:235
  69.6 35.1 %collective-permute-start.5 = (f32[1,1,2,2,104,640]{5,4,3,2,1,0:T(8,128)S(1)}, f32[1,1,2,2,104,640]{5,4,3,2,1,0:T(8,128)S(1)}, u32[]{:S(2)}, u32[]{:S(2)}) collective-permute-start(f32[1,1,2,2,104,640]{5,4,3,2,1,0:T(8,128)S(1)} %slice.119), channel_id=1, source_target_pairs={{0,4},{2,6},{4,0},{6,2},{8,12},{10,14},{12,8},{14,10},{16,20},{18,... | collective-permute-start | bytes 3194888 | tf_op jit(solution)/shard_map/ppermute | solution.py:236
  71.2 47.8 %collective-permute-start.6 = (f32[1,2,1,2,104,640]{5,4,3,2,1,0:T(8,128)S(1)}, f32[1,2,1,2,104,640]{5,4,3,2,1,0:T(8,128)S(1)}, u32[]{:S(2)}, u32[]{:S(2)}) collective-permute-start(f32[1,2,1,2,104,640]{5,4,3,2,1,0:T(8,128)S(1)} %slice.120), channel_id=1, source_target_pairs={{0,8},{2,10},{4,12},{6,14},{8,0},{10,2},{12,4},{14,6},{16,24},{18,... | collective-permute-start | bytes 3194888 | tf_op jit(solution)/shard_map/ppermute | solution.py:236
  79.9 39.2 %copy-start.1 = (f32[832,640]{1,0:T(8,128)}, f32[832,640]{1,0:T(8,128)S(1)}, u32[]{:S(2)}) copy-start(f32[832,640]{1,0:T(8,128)S(1)} %convolution_add_fusion.4) | copy-start | bytes 6389764
  120.4 37.3 %collective-permute-start.10 = (f32[1,1,2,2,104,640]{5,4,3,2,1,0:T(8,128)}, f32[1,1,2,2,104,640]{5,4,3,2,1,0:T(8,128)}, u32[]{:S(2)}, u32[]{:S(2)}) collective-permute-start(f32[1,1,2,2,104,640]{5,4,3,2,1,0:T(8,128)} %slice.121), channel_id=1, source_target_pairs={{0,4},{2,6},{4,0},{6,2},{8,12},{10,14},{12,8},{14,10},{16,20},{18,... | collective-permute-start | bytes 3194888 | tf_op jit(solution)/shard_map/ppermute | solution.py:236
  121.9 35.8 %collective-permute-start.8 = (f32[1,2,1,2,104,640]{5,4,3,2,1,0:T(8,128)}, f32[1,2,1,2,104,640]{5,4,3,2,1,0:T(8,128)}, u32[]{:S(2)}, u32[]{:S(2)}) collective-permute-start(f32[1,2,1,2,104,640]{5,4,3,2,1,0:T(8,128)} %get-tuple-element.55), channel_id=1, source_target_pairs={{0,1},{1,0},{2,3},{3,2},{4,5},{5,4},{6,7},{7,6},{8,9},{9,8},{10,11... | collective-permute-start | bytes 3194888 | tf_op jit(solution)/shard_map/ppermute | solution.py:235
  123.4 36.6 %collective-permute-start.9 = (f32[1,2,1,2,104,640]{5,4,3,2,1,0:T(8,128)}, f32[1,2,1,2,104,640]{5,4,3,2,1,0:T(8,128)}, u32[]{:S(2)}, u32[]{:S(2)}) collective-permute-start(f32[1,2,1,2,104,640]{5,4,3,2,1,0:T(8,128)} %slice_add_fusion.3), channel_id=1, source_target_pairs={{0,8},{2,10},{4,12},{6,14},{8,0},{10,2},{12,4},{14,6},{16,24},{18,... | collective-permute-start | bytes 3194888 | tf_op jit(solution)/shard_map/ppermute | solution.py:236
  123.4 34.3 %collective-permute-start.11 = (f32[1,2,1,1,104,640]{5,4,3,2,1,0:T(8,128)S(1)}, f32[1,2,1,1,104,640]{5,4,3,2,1,0:T(8,128)}, u32[]{:S(2)}, u32[]{:S(2)}) collective-permute-start(f32[1,2,1,1,104,640]{5,4,3,2,1,0:T(8,128)S(1)} %slice.123), channel_id=1, source_target_pairs={{0,16},{2,18},{4,20},{6,22},{8,24},{10,26},{12,28},{14,30},{16,0},... | collective-permute-start | bytes 1597448 | tf_op jit(solution)/shard_map/ppermute | solution.py:236
  126.3 33.7 %copy-start.13 = (f32[1,2,1,2,104,640]{5,4,3,2,1,0:T(8,128)S(1)}, f32[1,2,1,2,104,640]{5,4,3,2,1,0:T(8,128)}, u32[]{:S(2)}) copy-start(f32[1,2,1,2,104,640]{5,4,3,2,1,0:T(8,128)} %copy-done.12) | copy-start | bytes 3194884
  128.1 33.1 %copy-start.8 = (f32[1,1,2,2,104,640]{5,4,3,2,1,0:T(8,128)}, f32[1,1,2,2,104,640]{5,4,3,2,1,0:T(8,128)S(1)}, u32[]{:S(2)}) copy-start(f32[1,1,2,2,104,640]{5,4,3,2,1,0:T(8,128)S(1)} %slice_add_fusion.1) | copy-start | bytes 3194884
  128.1 33.8 %copy-start.7 = (f32[832,640]{1,0:T(8,128)S(1)}, f32[832,640]{1,0:T(8,128)}, u32[]{:S(2)}) copy-start(f32[832,640]{1,0:T(8,128)} %copy-done.6) | copy-start | bytes 6389764
  168.7 15.8 %copy-start.19 = (f32[1,1,1,2,104,640]{5,4,3,2,1,0:T(8,128)S(1)}, f32[1,1,1,2,104,640]{5,4,3,2,1,0:T(8,128)}, u32[]{:S(2)}) copy-start(f32[1,1,1,2,104,640]{5,4,3,2,1,0:T(8,128)} %slice.129) | copy-start | bytes 1597444
  168.7 16.1 %copy-start.21 = (f32[1,1,1,1,104,640]{5,4,3,2,1,0:T(8,128)S(1)}, f32[1,1,1,1,104,640]{5,4,3,2,1,0:T(8,128)}, u32[]{:S(2)}) copy-start(f32[1,1,1,1,104,640]{5,4,3,2,1,0:T(8,128)} %slice.131) | copy-start | bytes 798724
  168.7 16.6 %copy-start.29 = (bf16[1664,3200]{1,0:T(8,128)(2,1)S(1)}, bf16[1664,3200]{1,0:T(8,128)(2,1)}, u32[]{:S(2)}) copy-start(bf16[1664,3200]{1,0:T(8,128)(2,1)} %all-gather.2.cloned.1.call-done) | copy-start | bytes 31948804
  181.5 25.7 %collective-permute-start.12 = (f32[1,2,1,1,104,640]{5,4,3,2,1,0:T(8,128)S(1)}, f32[1,2,1,1,104,640]{5,4,3,2,1,0:T(8,128)S(1)}, u32[]{:S(2)}, u32[]{:S(2)}) collective-permute-start(f32[1,2,1,1,104,640]{5,4,3,2,1,0:T(8,128)S(1)} %copy-done.20), channel_id=1, source_target_pairs={{0,16},{2,18},{4,20},{6,22},{8,24},{10,26},{12,28},{14,30},{16,0},... | collective-permute-start | bytes 1597448 | tf_op jit(solution)/shard_map/ppermute | solution.py:236
  182.8 26.2 %collective-permute-start.13 = (f32[1,1,1,2,104,640]{5,4,3,2,1,0:T(8,128)S(1)}, f32[1,1,1,2,104,640]{5,4,3,2,1,0:T(8,128)S(1)}, u32[]{:S(2)}, u32[]{:S(2)}) collective-permute-start(f32[1,1,1,2,104,640]{5,4,3,2,1,0:T(8,128)S(1)} %copy-done.18), channel_id=1, source_target_pairs={{0,8},{2,10},{4,12},{6,14},{8,0},{10,2},{12,4},{14,6},{16,24},{18,... | collective-permute-start | bytes 1597448 | tf_op jit(solution)/shard_map/ppermute | solution.py:236
  184.5 34.1 %collective-permute-start.14 = (f32[1,1,1,2,104,640]{5,4,3,2,1,0:T(8,128)S(1)}, f32[1,1,1,2,104,640]{5,4,3,2,1,0:T(8,128)S(1)}, u32[]{:S(2)}, u32[]{:S(2)}) collective-permute-start(f32[1,1,1,2,104,640]{5,4,3,2,1,0:T(8,128)S(1)} %copy-done.19), channel_id=1, source_target_pairs={{0,8},{2,10},{4,12},{6,14},{8,0},{10,2},{12,4},{14,6},{16,24},{18,... | collective-permute-start | bytes 1597448 | tf_op jit(solution)/shard_map/ppermute | solution.py:236
  184.9 19.4 %collective-permute-start.15 = (f32[1,1,1,1,104,640]{5,4,3,2,1,0:T(8,128)S(1)}, f32[1,1,1,1,104,640]{5,4,3,2,1,0:T(8,128)S(1)}, u32[]{:S(2)}, u32[]{:S(2)}) collective-permute-start(f32[1,1,1,1,104,640]{5,4,3,2,1,0:T(8,128)S(1)} %copy-done.21), channel_id=1, source_target_pairs={{0,4},{2,6},{4,0},{6,2},{8,12},{10,14},{12,8},{14,10},{16,20},{18,... | collective-permute-start | bytes 798728 | tf_op jit(solution)/shard_map/ppermute | solution.py:236
  195.0 23.6 %copy-start.11 = (f32[1,1,2,2,104,640]{5,4,3,2,1,0:T(8,128)S(1)}, f32[1,1,2,2,104,640]{5,4,3,2,1,0:T(8,128)}, u32[]{:S(2)}) copy-start(f32[1,1,2,2,104,640]{5,4,3,2,1,0:T(8,128)} %copy-done.10) | copy-start | bytes 3194884
  221.1 29.4 %collective-permute-start.16 = (f32[1,1,1,1,104,640]{5,4,3,2,1,0:T(8,128)S(1)}, f32[1,1,1,1,104,640]{5,4,3,2,1,0:T(8,128)S(1)}, u32[]{:S(2)}, u32[]{:S(2)}) collective-permute-start(f32[1,1,1,1,104,640]{5,4,3,2,1,0:T(8,128)S(1)} %slice.133), channel_id=1, source_target_pairs={{0,4},{2,6},{4,0},{6,2},{8,12},{10,14},{12,8},{14,10},{16,20},{18,... | collective-permute-start | bytes 798728 | tf_op jit(solution)/shard_map/ppermute | solution.py:236
  221.7 28.9 %collective-permute-start.17 = (f32[1,1,1,1,104,640]{5,4,3,2,1,0:T(8,128)S(1)}, f32[1,1,1,1,104,640]{5,4,3,2,1,0:T(8,128)S(1)}, u32[]{:S(2)}, u32[]{:S(2)}) collective-permute-start(f32[1,1,1,1,104,640]{5,4,3,2,1,0:T(8,128)S(1)} %slice.135), channel_id=1, source_target_pairs={{0,16},{2,18},{4,20},{6,22},{8,24},{10,26},{12,28},{14,30},{16,0},... | collective-permute-start | bytes 798728 | tf_op jit(solution)/shard_map/ppermute | solution.py:236
  222.8 27.8 %collective-permute-start.18 = (f32[1,1,1,1,104,640]{5,4,3,2,1,0:T(8,128)S(1)}, f32[1,1,1,1,104,640]{5,4,3,2,1,0:T(8,128)S(1)}, u32[]{:S(2)}, u32[]{:S(2)}) collective-permute-start(f32[1,1,1,1,104,640]{5,4,3,2,1,0:T(8,128)S(1)} %slice.137), channel_id=1, source_target_pairs={{0,16},{2,18},{4,20},{6,22},{8,24},{10,26},{12,28},{14,30},{16,0},... | collective-permute-start | bytes 798728 | tf_op jit(solution)/shard_map/ppermute | solution.py:236
  224.6 26.0 %collective-permute-start.19 = (f32[1,1,1,1,104,640]{5,4,3,2,1,0:T(8,128)S(1)}, f32[1,1,1,1,104,640]{5,4,3,2,1,0:T(8,128)S(1)}, u32[]{:S(2)}, u32[]{:S(2)}) collective-permute-start(f32[1,1,1,1,104,640]{5,4,3,2,1,0:T(8,128)S(1)} %slice_add_fusion.11), channel_id=1, source_target_pairs={{0,1},{1,0},{2,3},{3,2},{4,5},{5,4},{6,7},{7,6},{8,9},{9,8},{10,11... | collective-permute-start | bytes 798728 | tf_op jit(solution)/shard_map/ppermute | solution.py:235
  250.7 25.0 %collective-permute-start.20 = (f32[1,1,1,1,104,640]{5,4,3,2,1,0:T(8,128)S(1)}, f32[1,1,1,1,104,640]{5,4,3,2,1,0:T(8,128)S(1)}, u32[]{:S(2)}, u32[]{:S(2)}) collective-permute-start(f32[1,1,1,1,104,640]{5,4,3,2,1,0:T(8,128)S(1)} %slice_add_fusion.12), channel_id=1, source_target_pairs={{0,1},{1,0},{2,3},{3,2},{4,5},{5,4},{6,7},{7,6},{8,9},{9,8},{10,11... | collective-permute-start | bytes 798728 | tf_op jit(solution)/shard_map/ppermute | solution.py:235
  252.3 23.5 %collective-permute-start.21 = (f32[1,1,1,1,104,640]{5,4,3,2,1,0:T(8,128)S(1)}, f32[1,1,1,1,104,640]{5,4,3,2,1,0:T(8,128)S(1)}, u32[]{:S(2)}, u32[]{:S(2)}) collective-permute-start(f32[1,1,1,1,104,640]{5,4,3,2,1,0:T(8,128)S(1)} %slice_add_fusion.10), channel_id=1, source_target_pairs={{0,1},{1,0},{2,3},{3,2},{4,5},{5,4},{6,7},{7,6},{8,9},{9,8},{10,11... | collective-permute-start | bytes 798728 | tf_op jit(solution)/shard_map/ppermute | solution.py:235
  252.8 22.9 %collective-permute-start.22 = (f32[1,1,1,1,104,640]{5,4,3,2,1,0:T(8,128)S(1)}, f32[1,1,1,1,104,640]{5,4,3,2,1,0:T(8,128)S(1)}, u32[]{:S(2)}, u32[]{:S(2)}) collective-permute-start(f32[1,1,1,1,104,640]{5,4,3,2,1,0:T(8,128)S(1)} %slice_add_fusion.9), channel_id=1, source_target_pairs={{0,1},{1,0},{2,3},{3,2},{4,5},{5,4},{6,7},{7,6},{8,9},{9,8},{10,11... | collective-permute-start | bytes 798728 | tf_op jit(solution)/shard_map/ppermute | solution.py:235
  (22 other events, 95.7 us)
Sparse Core Ops, SparseCore 0:
  10.2 107.3 all-gather.1

commit v3 on v2

--- a/solution.py
+++ b/solution.py
@@ -290,34 +290,27 @@
             array = low + across(high, bit)
         return array
 
-    (g_in, s_in, f_in), _ = together(
-        [(part_of(give, near, 1), -1), (part_of(second, x, 1), x), (part_of(fifth, near, 1), near)],
-        (),
-        nothing,
-    )
-    ahead = part_of(own, near, 1) + g_in
-    second = part_of(second, x, 0) + s_in
-    fifth = middle(part_of(fifth, near, 0) + f_in)
-    (g_in, a_in, t_in, f_in), _ = together(
+    (g_in, s_in, t_in, f_in), _ = together(
         [
-            (part_of(give, near, 0), -1),
-            (ahead, near),
+            (give, -1),
+            (part_of(second, x, 1), x),
             (part_of(third, x, 1), x),
-            (part_of(fifth, last, 1), last),
+            (part_of(fifth, near, 1), near),
         ],
         (),
         nothing,
     )
-    own = middle(part_of(own, near, 0) + g_in + a_in)
+    own = own + g_in
+    second = part_of(second, x, 0) + s_in
     third = part_of(third, x, 0) + t_in
-    fifth = part_of(fifth, last, 0) + f_in
+    fifth = middle(part_of(fifth, near, 0) + f_in)
 
     def grad_of(weight):
         return lax.dot_general(
             weight, masked_cot, (((1,), (1,)), ((), ())), preferred_element_type=jnp.float32
         ).astype(jnp.bfloat16)
 
-    cuts = (0, heads * 2 // 13, heads * 8 // 13, heads)
+    cuts = (0, heads * 5 // 13, heads * 11 // 13, heads)
 
     def backward(grad_t, index, before):
         return attention_backward(
@@ -328,49 +321,57 @@
         grad_t = grad_of(weight)
         return grad_t, backward(grad_t, 0, None)
 
+    (o_in, s_in, f_in), (grad_t, grad_projected) = together(
+        [
+            (part_of(own, near, 1), near),
+            (part_of(second, near, 1), near),
+            (part_of(fifth, last, 1), last),
+        ],
+        full_weight,
+        work_one,
+    )
+    own = middle(part_of(own, near, 0) + o_in)
+    second = middle(part_of(second, near, 0) + s_in)
+    fifth = part_of(fifth, last, 0) + f_in
     (o_in, s_in, t_in, f_in), (grad_t, grad_projected) = together(
         [
             (part_of(own, last, 1), last),
-            (part_of(second, near, 1), near),
+            (part_of(second, last, 1), last),
             (part_of(third, near, 1), near),
             (part_of(fifth, x, 1), x),
         ],
-        full_weight,
-        work_one,
+        (grad_t, grad_projected),
+        lambda held: (held[0], backward(held[0], 1, held[1])),
     )
     own = part_of(own, last, 0) + o_in
-    second = middle(part_of(second, near, 0) + s_in)
+    second = part_of(second, last, 0) + s_in
     third = middle(part_of(third, near, 0) + t_in)
     fifth = part_of(fifth, x, 0) + f_in
-    (o_in, s_in, t_in, f_in), (grad_t, grad_projected) = together(
+    (o_in, s_in, t_in, f_in), grad_projected = together(
         [
             (part_of(own, x, 1), x),
-            (part_of(second, last, 1), last),
+            (second, -1),
             (part_of(third, last, 1), last),
             (fifth, -1),
         ],
         (grad_t, grad_projected),
-        lambda held: (held[0], backward(held[0], 1, held[1])),
+        lambda held: backward(held[0], 2, held[1]),
     )
     own = part_of(own, x, 0) + o_in
-    second = part_of(second, last, 0) + s_in
+    second = second + s_in
     third = part_of(third, last, 0) + t_in
     fifth = fifth + f_in
-
-    def work_last(held):
-        grad_t, grad_projected = held
-        out = lax.dot_general(
-            attn_t, full_weight, (((0,), (0,)), ((), ())), preferred_element_type=jnp.float32
-        ).astype(jnp.bfloat16)
-        return out, backward(grad_t, 2, grad_projected)
-
-    (o_in, s_in, t_in), (work_out, grad_projected) = together(
-        [(own, -1), (second, -1), (third, -1)], (grad_t, grad_projected), work_last
+    (o_in, t_in), work_out = together(
+        [(own, -1), (third, -1)],
+        (attn_t, full_weight),
+        lambda held: lax.dot_general(
+            held[0], held[1], (((0,), (0,)), ((), ())), preferred_element_type=jnp.float32
+        ).astype(jnp.bfloat16),
     )
     pieces = [
         jnp.where(row_side == 0, own, o_in),
         jnp.where(row_side == 0, o_in, own),
-        second + s_in,
+        second,
         third + t_in,
         fifth,
     ]

time: 285 us -> 265 us (0.930)
  waiting for transfers between devices: 84.4 us -> 62.6 us
  matrix products: 52.7 us -> 58.2 us
    ppermute x6 -> x5, waiting for transfers between devices: 13.8 us -> 0.01 us  [across(): return lax.ppermute(array, 'dp', [(i, i ^ 1) for i in range(pair)])]
    ppermute x17, waiting for transfers between devices: 70.6 us -> 62.5 us  [across(): lax.ppermute(array, 'fsdp', [(i, i ^ 1 << bit) for i in range(devices)])]
    dot_general x1, matrix products: 9.65 us -> 12.6 us  [body(): lax.dot_general(held[0], held[1], (((0,), (0,)), ((), ())), preferred_ele...]
    unnamed x67 -> x55, local copies, waits for them, and re-layouts: 12 us -> 10.5 us
    ppermute x6 -> x5, starting transfers between devices: 8.04 us -> 6.58 us  [across(): return lax.ppermute(array, 'dp', [(i, i ^ 1) for i in range(pair)])]
  transfers between devices with their start and end apart: 24 -> 23, of which waited for: 8 -> 5; matrix products, arithmetic and copies ran while one was open for 22% -> 31% of each run, Pallas kernels for 26% -> 28%
where the time goes in v3:
time: 265 us; the launch traced here: 264 us
  Pallas kernels  74.9 us (28%)
  waiting for transfers between devices  62.6 us (24%)
  matrix products  58.2 us (22%)
  starting transfers between devices  22.6 us (9%)
  local copies, waits for them, and re-layouts  17.7 us (7%)
  between operations  14.8 us (6%)
  other arithmetic  13.4 us (5%)
    ppermute x17, waiting for transfers between devices, across(): lax.ppermute(array, 'fsdp', [(i, i ^ 1 << bit) for i in range(devices)])  62.5 us
    pallas_call x3, Pallas kernels, attention_backward(): pl.pallas_call(kernel, grid_spec=pltpu.PrefetchScalarGridSpec(num_scalar_...  56.2 us
    dot_general x10, matrix products, product(): return jnp.dot(left, cot, preferred_element_type=jnp.float32)  33 us
    pallas_call x1, Pallas kernels, attention_forward(): pl.pallas_call(forward_kernel, grid_spec=pltpu.PrefetchScalarGridSpec(num...  18.7 us
    ppermute x17, starting transfers between devices, across(): lax.ppermute(array, 'fsdp', [(i, i ^ 1 << bit) for i in range(devices)])  16 us
    dot_general x1, matrix products, grad_of(): lax.dot_general(weight, masked_cot, (((1,), (1,)), ((), ())), preferred_e...  12.6 us
    dot_general x1, matrix products, body(): lax.dot_general(held[0], held[1], (((0,), (0,)), ((), ())), preferred_ele...  12.6 us
    unnamed x55, local copies, waits for them, and re-layouts  10.5 us
  transfers between devices with their start and end apart: 23, of which 5 were waited for; matrix products, arithmetic and copies ran while one was open for 31% of the time, Pallas kernels for 28%

profile of v3, /device:TPU:0, one launch (start us, length us, event | category | flops | bytes accessed | tf_op | source)
XLA Modules:
  0.0 264.3 jit_solution(14764997431940463630)
XLA Ops:
  7.3 2.2 convert_element_type.29
  11.0 2.4 fusion.17
  13.6 18.7 %shard_map.94 = bf16[1664,640]{1,0:T(8,128)(2,1)S(1)} custom-call(s32[2]{0:T(128)S(1)} %copy-done, bf16[640,4992]{1,0:T(8,128)(2,1)} %refs_3_.3, bf16[640,4992]{1,0:T(8,128)(2,1)} %refs_3_.3, bf16[640,4992]{1,0:T(8,128)(2,1)} %refs_3_.3, f32[640,128]{1,0:T(8,128)S(1)} %get-tuple-element.119.cos_ref.refs_5_, f32[640,128]{1,0:T(8,128)S(1)} %get-tuple-element.120.sin_ref.refs_6_), custom_call_target="tpu_custom_call" | custom-call | flops 4089446400 | bytes 8519680 | tf_op jit(solution)/shard_map/pallas_call | solution.py:144
  38.3 2.7 %fusion.6 = f32[832,640]{1,0:T(8,128)} fusion(bf16[832,640]{1,0:T(8,128)(2,1)S(1)} %get-tuple-element.98, bf16[640,3200]{1,0:T(8,128)(2,1)S(1)} %broadcast_multiply_fusion), kind=kOutput, calls=%fused_computation.18 | convolution fusion | flops 681574400 | bytes 4014080 | tf_op jit(solution)/shard_map/dot_general | solution.py:267
  41.4 2.5 fusion.3
  44.0 2.4 fusion
  46.9 3.9 %fusion.9 = f32[832,640]{1,0:T(8,128)} fusion(bf16[832,640]{1,0:T(8,128)(2,1)} %copy-done.19, bf16[640,3200]{1,0:T(8,128)(2,1)} %copy-done.1, s32[]{:T(128)S(6)} %select_n.118), kind=kOutput, calls=%fused_computation.21 | convolution fusion | flops 681574400 | bytes 4014084 | tf_op jit(solution)/shard_map/dot_general | solution.py:267
  50.8 4.6 %fusion.12 = f32[832,640]{1,0:T(8,128)} fusion(bf16[832,640]{1,0:T(8,128)(2,1)} %copy-done.19, bf16[640,3200]{1,0:T(8,128)(2,1)} %copy-done.1, s32[]{:T(128)S(6)} %select_n.109), kind=kOutput, calls=%fused_computation.24 | convolution fusion | flops 681574400 | bytes 4014084 | tf_op jit(solution)/shard_map/dot_general | solution.py:267
  55.9 3.1 %convolution_add_fusion.2 = f32[832,640]{1,0:T(8,128)S(1)} fusion(f32[832,640]{1,0:T(8,128)} %collective-permute-done.2, bf16[832,640]{1,0:T(8,128)(2,1)} %get-tuple-element.97, bf16[640,3200]{1,0:T(8,128)(2,1)S(1)} %copy-done.2), kind=kOutput, calls=%fused_computation.5 | convolution fusion | flops 682106880 | bytes 6144000 | tf_op jit(solution)/shard_map/dot_general | solution.py:267
  60.7 3.1 %convolution_add_fusion.1 = f32[832,640]{1,0:T(8,128)S(1)} fusion(f32[832,640]{1,0:T(8,128)} %collective-permute-done.3, bf16[832,640]{1,0:T(8,128)(2,1)} %get-tuple-element.97, bf16[640,3200]{1,0:T(8,128)(2,1)S(1)} %copy-done.2), kind=kOutput, calls=%fused_computation.4 | convolution fusion | flops 682106880 | bytes 6144000 | tf_op jit(solution)/shard_map/dot_general | solution.py:267
  64.9 3.0 %convolution_add_fusion = f32[832,640]{1,0:T(8,128)S(1)} fusion(f32[832,640]{1,0:T(8,128)} %collective-permute-done.4, bf16[832,640]{1,0:T(8,128)(2,1)} %get-tuple-element.97, bf16[640,3200]{1,0:T(8,128)(2,1)S(1)} %copy-done.2), kind=kOutput, calls=%fused_computation.3 | convolution fusion | flops 682106880 | bytes 6144000 | tf_op jit(solution)/shard_map/dot_general | solution.py:267
  69.2 4.4 %convolution_add_fusion.3 = f32[832,640]{1,0:T(8,128)} fusion(f32[832,640]{1,0:T(8,128)} %collective-permute-done.1, bf16[832,640]{1,0:T(8,128)(2,1)} %get-tuple-element.97, bf16[640,3200]{1,0:T(8,128)(2,1)S(1)} %copy-done.2, s32[]{:T(128)S(6)} %select_n.118), kind=kOutput, calls=%fused_computation.6 | convolution fusion | flops 682106880 | bytes 6144004 | tf_op jit(solution)/shard_map/dot_general | solution.py:267
  73.6 2.5 collective-permute-start.5
  78.1 1.6 collective-permute-start.8
  79.6 3.3 %convolution_add_fusion.4 = f32[832,640]{1,0:T(8,128)S(1)} fusion(f32[832,640]{1,0:T(8,128)} %collective-permute-done, bf16[832,640]{1,0:T(8,128)(2,1)} %get-tuple-element.97, bf16[640,3200]{1,0:T(8,128)(2,1)} %copy-done.1, s32[]{:T(128)S(6)} %select_n.109), kind=kOutput, calls=%fused_computation.7 | convolution fusion | flops 682106880 | bytes 6144004 | tf_op jit(solution)/shard_map/dot_general | solution.py:267
  82.9 22.3 %collective-permute-done.6 = f32[1,1,2,2,104,640]{5,4,3,2,1,0:T(8,128)} collective-permute-done((f32[1,1,2,2,104,640]{5,4,3,2,1,0:T(8,128)}, f32[1,1,2,2,104,640]{5,4,3,2,1,0:T(8,128)}, u32[]{:S(2)}, u32[]{:S(2)}) %collective-permute-start.6) | collective-permute-done | bytes 1064992 | tf_op jit(solution)/shard_map/ppermute | solution.py:236
  105.2 22.4 %collective-permute-done.7 = f32[1,1,2,2,104,640]{5,4,3,2,1,0:T(8,128)} collective-permute-done((f32[1,1,2,2,104,640]{5,4,3,2,1,0:T(8,128)}, f32[1,1,2,2,104,640]{5,4,3,2,1,0:T(8,128)}, u32[]{:S(2)}, u32[]{:S(2)}) %collective-permute-start.7) | collective-permute-done | bytes 1064992 | tf_op jit(solution)/shard_map/ppermute | solution.py:236
  127.6 1.8 add.156
  130.6 1.7 copy-done.6
  141.8 2.4 collective-permute-start.11
  144.2 12.6 %convolution_convert_fusion.1.g_ref.refs_4_ = bf16[1664,640]{1,0:T(8,128)(2,1)S(1)} fusion(bf16[1664,3200]{1,0:T(8,128)(2,1)} %all-gather.2.cloned.1.call-done, bf16[640,3200]{1,0:T(8,128)(2,1)} %copy-done.1), kind=kOutput, calls=%fused_computation.1 | convolution fusion | flops 6816808960 | bytes 16875520 | tf_op jit(solution)/shard_map/dot_general | solution.py:309
  156.9 21.5 %shard_map.95.refs_7_ = bf16[640,4992]{1,0:T(8,128)(2,1)} custom-call(s32[2]{0:T(128)S(1)} %copy-done, bf16[640,4992]{1,0:T(8,128)(2,1)} %refs_3_.3, bf16[640,4992]{1,0:T(8,128)(2,1)} %refs_3_.3, bf16[640,4992]{1,0:T(8,128)(2,1)} %refs_3_.3, bf16[1664,640]{1,0:T(8,128)(2,1)S(1)} %convolution_convert_fusion.1.g_ref.refs_4_, ...), custom_call_target="tpu_custom_call" | custom-call | flops 18350080000 | bytes 5734400 | tf_op jit(solution)/shard_map/pallas_call | solution.py:196
  178.4 9.6 %collective-permute-done.10 = f32[1,1,1,2,104,640]{5,4,3,2,1,0:T(8,128)S(1)} collective-permute-done((f32[1,1,1,2,104,640]{5,4,3,2,1,0:T(8,128)}, f32[1,1,1,2,104,640]{5,4,3,2,1,0:T(8,128)S(1)}, u32[]{:S(2)}, u32[]{:S(2)}) %collective-permute-start.10) | collective-permute-done | bytes 532512 | tf_op jit(solution)/shard_map/ppermute | solution.py:236
  189.7 2.4 collective-permute-start.12
  192.7 2.4 collective-permute-start.14
  195.7 25.5 %shard_map.96.refs_7_ = bf16[640,4992]{1,0:T(8,128)(2,1)} custom-call(s32[2]{0:T(128)S(1)} %copy-done, bf16[640,4992]{1,0:T(8,128)(2,1)} %refs_3_.3, bf16[640,4992]{1,0:T(8,128)(2,1)} %refs_3_.3, bf16[640,4992]{1,0:T(8,128)(2,1)} %refs_3_.3, bf16[1664,640]{1,0:T(8,128)(2,1)S(1)} %convolution_convert_fusion.1.g_ref.refs_4_, ...), custom_call_target="tpu_custom_call", output_to_operand_aliasing={{}: (7, {})} | custom-call | flops 22020096000 | bytes 6881280 | tf_op jit(solution)/shard_map/pallas_call | solution.py:196
  221.2 5.1 %collective-permute-done.13 = f32[1,1,1,1,104,640]{5,4,3,2,1,0:T(8,128)S(1)} collective-permute-done((f32[1,1,1,1,104,640]{5,4,3,2,1,0:T(8,128)S(1)}, f32[1,1,1,1,104,640]{5,4,3,2,1,0:T(8,128)S(1)}, u32[]{:S(2)}, u32[]{:S(2)}) %collective-permute-start.13) | collective-permute-done | bytes 266272 | tf_op jit(solution)/shard_map/ppermute | solution.py:236
  227.0 1.7 collective-permute-start.17
  229.0 9.3 %shard_map.97 = bf16[640,4992]{1,0:T(8,128)(2,1)} custom-call(s32[2]{0:T(128)S(1)} %copy-done, bf16[640,4992]{1,0:T(8,128)(2,1)} %refs_3_.3, bf16[640,4992]{1,0:T(8,128)(2,1)} %refs_3_.3, bf16[640,4992]{1,0:T(8,128)(2,1)} %refs_3_.3, bf16[1664,640]{1,0:T(8,128)(2,1)S(1)} %convolution_convert_fusion.1.g_ref.refs_4_, ...), custom_call_target="tpu_custom_call", output_to_operand_aliasing={{}: (7, {})} | custom-call | flops 7340032000 | bytes 2293760 | tf_op jit(solution)/shard_map/pallas_call | solution.py:196
  238.3 3.0 %collective-permute-done.18 = f32[1,1,1,1,104,640]{5,4,3,2,1,0:T(8,128)S(1)} collective-permute-done((f32[1,1,1,1,104,640]{5,4,3,2,1,0:T(8,128)S(1)}, f32[1,1,1,1,104,640]{5,4,3,2,1,0:T(8,128)S(1)}, u32[]{:S(2)}, u32[]{:S(2)}) %collective-permute-start.18) | collective-permute-done | bytes 266272 | tf_op jit(solution)/shard_map/ppermute | solution.py:236
  241.9 1.7 collective-permute-start.21
  243.5 12.6 %convolution_convert_fusion = bf16[640,3200]{1,0:T(8,128)(2,1)} fusion(bf16[1664,640]{1,0:T(8,128)(2,1)S(1)} %shard_map.94, bf16[1664,3200]{1,0:T(8,128)(2,1)} %all-gather.2.cloned.1.call-done), kind=kOutput, calls=%fused_computation | convolution fusion | flops 6817792000 | bytes 16875520 | tf_op jit(solution)/shard_map/dot_general | solution.py:367
  (124 shorter events, 31.0 us)
Async XLA Ops:
  7.2 132.3 %all-gather.2.cloned.1.call-start = ((), (), s32[]{:S(2)}) async-start(), calls=%async_computation | async-start | bytes 11315200 | tf_op jit(solution)/shard_map/all_gather | solution.py:254
  32.3 5.5 %copy-start.17 = (bf16[640,3200]{1,0:T(8,128)(2,1)S(1)}, bf16[640,3200]{1,0:T(8,128)(2,1)}, u32[]{:S(2)}) copy-start(bf16[640,3200]{1,0:T(8,128)(2,1)} %param.8) | copy-start | bytes 12288004
  37.8 6.2 %copy-start.19 = (bf16[832,640]{1,0:T(8,128)(2,1)}, bf16[832,640]{1,0:T(8,128)(2,1)S(1)}, u32[]{:S(2)}) copy-start(bf16[832,640]{1,0:T(8,128)(2,1)S(1)} %get-tuple-element.98) | copy-start | bytes 3194884
  38.3 5.7 %copy-start.1 = (bf16[640,3200]{1,0:T(8,128)(2,1)}, bf16[640,3200]{1,0:T(8,128)(2,1)S(1)}, u32[]{:S(2)}) copy-start(bf16[640,3200]{1,0:T(8,128)(2,1)S(1)} %broadcast_multiply_fusion) | copy-start | bytes 12288004
  40.9 15.0 %collective-permute-start.2 = (f32[832,640]{1,0:T(8,128)}, f32[832,640]{1,0:T(8,128)}, u32[]{:S(2)}, u32[]{:S(2)}) collective-permute-start(f32[832,640]{1,0:T(8,128)} %fusion.6), channel_id=1, source_target_pairs={{0,2},{2,0},{4,6},{6,4},{8,10},{10,8},{12,14},{14,12},{16,18},{18,... | collective-permute-start | bytes 6389768 | tf_op jit(solution)/shard_map/ppermute | solution.py:236
  43.9 16.8 %collective-permute-start.3 = (f32[832,640]{1,0:T(8,128)}, f32[832,640]{1,0:T(8,128)}, u32[]{:S(2)}, u32[]{:S(2)}) collective-permute-start(f32[832,640]{1,0:T(8,128)} %fusion.3), channel_id=1, source_target_pairs={{0,2},{2,0},{4,6},{6,4},{8,10},{10,8},{12,14},{14,12},{16,18},{18,... | collective-permute-start | bytes 6389768 | tf_op jit(solution)/shard_map/ppermute | solution.py:236
  46.4 18.5 %collective-permute-start.4 = (f32[832,640]{1,0:T(8,128)}, f32[832,640]{1,0:T(8,128)}, u32[]{:S(2)}, u32[]{:S(2)}) collective-permute-start(f32[832,640]{1,0:T(8,128)} %fusion), channel_id=1, source_target_pairs={{0,2},{2,0},{4,6},{6,4},{8,10},{10,8},{12,14},{14,12},{16,18},{18,... | collective-permute-start | bytes 6389768 | tf_op jit(solution)/shard_map/ppermute | solution.py:236
  50.8 18.4 %collective-permute-start.1 = (f32[832,640]{1,0:T(8,128)}, f32[832,640]{1,0:T(8,128)}, u32[]{:S(2)}, u32[]{:S(2)}) collective-permute-start(f32[832,640]{1,0:T(8,128)} %fusion.9), channel_id=1, source_target_pairs={{0,2},{2,0},{4,6},{6,4},{8,10},{10,8},{12,14},{14,12},{16,18},{18,... | collective-permute-start | bytes 6389768 | tf_op jit(solution)/shard_map/ppermute | solution.py:236
  50.8 5.1 %copy-start.2 = (bf16[640,3200]{1,0:T(8,128)(2,1)S(1)}, bf16[640,3200]{1,0:T(8,128)(2,1)}, u32[]{:S(2)}) copy-start(bf16[640,3200]{1,0:T(8,128)(2,1)} %copy-done.1) | copy-start | bytes 12288004
  55.4 24.2 %collective-permute-start = (f32[832,640]{1,0:T(8,128)}, f32[832,640]{1,0:T(8,128)}, u32[]{:S(2)}, u32[]{:S(2)}) collective-permute-start(f32[832,640]{1,0:T(8,128)} %fusion.12), channel_id=1, source_target_pairs={{0,2},{2,0},{4,6},{6,4},{8,10},{10,8},{12,14},{14,12},{16,18},{18,... | collective-permute-start | bytes 6389768 | tf_op jit(solution)/shard_map/ppermute | solution.py:236
  63.8 4.2 %copy-start.3 = (f32[832,640]{1,0:T(8,128)}, f32[832,640]{1,0:T(8,128)S(1)}, u32[]{:S(2)}) copy-start(f32[832,640]{1,0:T(8,128)S(1)} %convolution_add_fusion.1) | copy-start | bytes 6389764
  67.9 5.6 %copy-start.7 = (f32[832,640]{1,0:T(8,128)}, f32[832,640]{1,0:T(8,128)S(1)}, u32[]{:S(2)}) copy-start(f32[832,640]{1,0:T(8,128)S(1)} %convolution_add_fusion) | copy-start | bytes 6389764
  73.6 54.1 %collective-permute-start.5 = (f32[1,2,2,2,104,640]{5,4,3,2,1,0:T(8,128)}, f32[1,2,2,2,104,640]{5,4,3,2,1,0:T(8,128)}, u32[]{:S(2)}, u32[]{:S(2)}) collective-permute-start(f32[1,2,2,2,104,640]{5,4,3,2,1,0:T(8,128)} %bitcast.1), channel_id=1, source_target_pairs={{0,1},{1,0},{2,3},{3,2},{4,5},{5,4},{6,7},{7,6},{8,9},{9,8},{10,11... | collective-permute-start | bytes 6389768 | tf_op jit(solution)/shard_map/ppermute | solution.py:235
  76.0 29.2 %collective-permute-start.6 = (f32[1,1,2,2,104,640]{5,4,3,2,1,0:T(8,128)}, f32[1,1,2,2,104,640]{5,4,3,2,1,0:T(8,128)}, u32[]{:S(2)}, u32[]{:S(2)}) collective-permute-start(f32[1,1,2,2,104,640]{5,4,3,2,1,0:T(8,128)} %slice.107), channel_id=1, source_target_pairs={{0,4},{2,6},{4,0},{6,2},{8,12},{10,14},{12,8},{14,10},{16,20},{18,... | collective-permute-start | bytes 3194888 | tf_op jit(solution)/shard_map/ppermute | solution.py:236
  77.5 50.1 %collective-permute-start.7 = (f32[1,1,2,2,104,640]{5,4,3,2,1,0:T(8,128)}, f32[1,1,2,2,104,640]{5,4,3,2,1,0:T(8,128)}, u32[]{:S(2)}, u32[]{:S(2)}) collective-permute-start(f32[1,1,2,2,104,640]{5,4,3,2,1,0:T(8,128)} %slice.108), channel_id=1, source_target_pairs={{0,4},{2,6},{4,0},{6,2},{8,12},{10,14},{12,8},{14,10},{16,20},{18,... | collective-permute-start | bytes 3194888 | tf_op jit(solution)/shard_map/ppermute | solution.py:236
  78.1 49.6 %collective-permute-start.8 = (f32[1,2,1,2,104,640]{5,4,3,2,1,0:T(8,128)}, f32[1,2,1,2,104,640]{5,4,3,2,1,0:T(8,128)}, u32[]{:S(2)}, u32[]{:S(2)}) collective-permute-start(f32[1,2,1,2,104,640]{5,4,3,2,1,0:T(8,128)} %slice.109), channel_id=1, source_target_pairs={{0,8},{2,10},{4,12},{6,14},{8,0},{10,2},{12,4},{14,6},{16,24},{18,... | collective-permute-start | bytes 3194888 | tf_op jit(solution)/shard_map/ppermute | solution.py:236
  129.5 4.3 %copy-start.9 = (f32[1,2,2,2,104,640]{5,4,3,2,1,0:T(8,128)}, f32[1,2,2,2,104,640]{5,4,3,2,1,0:T(8,128)S(1)}, u32[]{:S(2)}) copy-start(f32[1,2,2,2,104,640]{5,4,3,2,1,0:T(8,128)S(1)} %add.156) | copy-start | bytes 6389764
  139.7 48.2 %collective-permute-start.9 = (f32[1,2,1,2,104,640]{5,4,3,2,1,0:T(8,128)}, f32[1,2,1,2,104,640]{5,4,3,2,1,0:T(8,128)S(1)}, u32[]{:S(2)}, u32[]{:S(2)}) collective-permute-start(f32[1,2,1,2,104,640]{5,4,3,2,1,0:T(8,128)} %slice.111), channel_id=1, source_target_pairs={{0,8},{2,10},{4,12},{6,14},{8,0},{10,2},{12,4},{14,6},{16,24},{18,... | collective-permute-start | bytes 3194888 | tf_op jit(solution)/shard_map/ppermute | solution.py:236
  141.3 46.7 %collective-permute-start.10 = (f32[1,1,1,2,104,640]{5,4,3,2,1,0:T(8,128)}, f32[1,1,1,2,104,640]{5,4,3,2,1,0:T(8,128)S(1)}, u32[]{:S(2)}, u32[]{:S(2)}) collective-permute-start(f32[1,1,1,2,104,640]{5,4,3,2,1,0:T(8,128)} %slice.113), channel_id=1, source_target_pairs={{0,8},{2,10},{4,12},{6,14},{8,0},{10,2},{12,4},{14,6},{16,24},{18,... | collective-permute-start | bytes 1597448 | tf_op jit(solution)/shard_map/ppermute | solution.py:236
  141.8 46.1 %collective-permute-start.11 = (f32[1,2,1,1,104,640]{5,4,3,2,1,0:T(8,128)}, f32[1,2,1,1,104,640]{5,4,3,2,1,0:T(8,128)S(1)}, u32[]{:S(2)}, u32[]{:S(2)}) collective-permute-start(f32[1,2,1,1,104,640]{5,4,3,2,1,0:T(8,128)} %slice.115), channel_id=1, source_target_pairs={{0,16},{2,18},{4,20},{6,22},{8,24},{10,26},{12,28},{14,30},{16,0},... | collective-permute-start | bytes 1597448 | tf_op jit(solution)/shard_map/ppermute | solution.py:236
  156.9 31.1 %copy-start.10 = (f32[1,2,2,2,104,640]{5,4,3,2,1,0:T(8,128)S(1)}, f32[1,2,2,2,104,640]{5,4,3,2,1,0:T(8,128)}, u32[]{:S(2)}) copy-start(f32[1,2,2,2,104,640]{5,4,3,2,1,0:T(8,128)} %copy-done.9) | copy-start | bytes 6389764
  189.7 36.6 %collective-permute-start.12 = (f32[1,2,1,1,104,640]{5,4,3,2,1,0:T(8,128)S(1)}, f32[1,2,1,1,104,640]{5,4,3,2,1,0:T(8,128)S(1)}, u32[]{:S(2)}, u32[]{:S(2)}) collective-permute-start(f32[1,2,1,1,104,640]{5,4,3,2,1,0:T(8,128)S(1)} %slice.117), channel_id=1, source_target_pairs={{0,16},{2,18},{4,20},{6,22},{8,24},{10,26},{12,28},{14,30},{16,0},... | collective-permute-start | bytes 1597448 | tf_op jit(solution)/shard_map/ppermute | solution.py:236
  192.1 34.2 %collective-permute-start.13 = (f32[1,1,1,1,104,640]{5,4,3,2,1,0:T(8,128)S(1)}, f32[1,1,1,1,104,640]{5,4,3,2,1,0:T(8,128)S(1)}, u32[]{:S(2)}, u32[]{:S(2)}) collective-permute-start(f32[1,1,1,1,104,640]{5,4,3,2,1,0:T(8,128)S(1)} %slice.119), channel_id=1, source_target_pairs={{0,16},{2,18},{4,20},{6,22},{8,24},{10,26},{12,28},{14,30},{16,0},... | collective-permute-start | bytes 798728 | tf_op jit(solution)/shard_map/ppermute | solution.py:236
  192.7 33.6 %collective-permute-start.14 = (f32[1,1,1,2,104,640]{5,4,3,2,1,0:T(8,128)S(1)}, f32[1,1,1,2,104,640]{5,4,3,2,1,0:T(8,128)S(1)}, u32[]{:S(2)}, u32[]{:S(2)}) collective-permute-start(f32[1,1,1,2,104,640]{5,4,3,2,1,0:T(8,128)S(1)} %slice.121), channel_id=1, source_target_pairs={{0,8},{2,10},{4,12},{6,14},{8,0},{10,2},{12,4},{14,6},{16,24},{18,... | collective-permute-start | bytes 1597448 | tf_op jit(solution)/shard_map/ppermute | solution.py:236
  195.1 31.2 %collective-permute-start.15 = (f32[1,1,1,1,104,640]{5,4,3,2,1,0:T(8,128)S(1)}, f32[1,1,1,1,104,640]{5,4,3,2,1,0:T(8,128)S(1)}, u32[]{:S(2)}, u32[]{:S(2)}) collective-permute-start(f32[1,1,1,1,104,640]{5,4,3,2,1,0:T(8,128)S(1)} %slice.123), channel_id=1, source_target_pairs={{0,4},{2,6},{4,0},{6,2},{8,12},{10,14},{12,8},{14,10},{16,20},{18,... | collective-permute-start | bytes 798728 | tf_op jit(solution)/shard_map/ppermute | solution.py:236
  221.2 5.3 %copy-start.12 = (f32[1,1,2,2,104,640]{5,4,3,2,1,0:T(8,128)S(1)}, f32[1,1,2,2,104,640]{5,4,3,2,1,0:T(8,128)}, u32[]{:S(2)}) copy-start(f32[1,1,2,2,104,640]{5,4,3,2,1,0:T(8,128)} %copy-done.11) | copy-start | bytes 3194884
  226.6 11.7 %collective-permute-start.16 = (f32[1,1,1,1,104,640]{5,4,3,2,1,0:T(8,128)S(1)}, f32[1,1,1,1,104,640]{5,4,3,2,1,0:T(8,128)S(1)}, u32[]{:S(2)}, u32[]{:S(2)}) collective-permute-start(f32[1,1,1,1,104,640]{5,4,3,2,1,0:T(8,128)S(1)} %slice.125), channel_id=1, source_target_pairs={{0,4},{2,6},{4,0},{6,2},{8,12},{10,14},{12,8},{14,10},{16,20},{18,... | collective-permute-start | bytes 798728 | tf_op jit(solution)/shard_map/ppermute | solution.py:236
  227.0 11.3 %collective-permute-start.17 = (f32[1,1,1,1,104,640]{5,4,3,2,1,0:T(8,128)S(1)}, f32[1,1,1,1,104,640]{5,4,3,2,1,0:T(8,128)S(1)}, u32[]{:S(2)}, u32[]{:S(2)}) collective-permute-start(f32[1,1,1,1,104,640]{5,4,3,2,1,0:T(8,128)S(1)} %slice_add_fusion.10), channel_id=1, source_target_pairs={{0,1},{1,0},{2,3},{3,2},{4,5},{5,4},{6,7},{7,6},{8,9},{9,8},{10,11... | collective-permute-start | bytes 798728 | tf_op jit(solution)/shard_map/ppermute | solution.py:235
  228.7 12.6 %collective-permute-start.18 = (f32[1,1,1,1,104,640]{5,4,3,2,1,0:T(8,128)S(1)}, f32[1,1,1,1,104,640]{5,4,3,2,1,0:T(8,128)S(1)}, u32[]{:S(2)}, u32[]{:S(2)}) collective-permute-start(f32[1,1,1,1,104,640]{5,4,3,2,1,0:T(8,128)S(1)} %slice.128), channel_id=1, source_target_pairs={{0,16},{2,18},{4,20},{6,22},{8,24},{10,26},{12,28},{14,30},{16,0},... | collective-permute-start | bytes 798728 | tf_op jit(solution)/shard_map/ppermute | solution.py:236
  228.7 12.6 %collective-permute-start.19 = (f32[1,1,1,1,104,640]{5,4,3,2,1,0:T(8,128)S(1)}, f32[1,1,1,1,104,640]{5,4,3,2,1,0:T(8,128)S(1)}, u32[]{:S(2)}, u32[]{:S(2)}) collective-permute-start(f32[1,1,1,1,104,640]{5,4,3,2,1,0:T(8,128)S(1)} %slice_add_fusion.9), channel_id=1, source_target_pairs={{0,1},{1,0},{2,3},{3,2},{4,5},{5,4},{6,7},{7,6},{8,9},{9,8},{10,11... | collective-permute-start | bytes 798728 | tf_op jit(solution)/shard_map/ppermute | solution.py:235
  241.4 14.7 %collective-permute-start.20 = (f32[1,1,1,1,104,640]{5,4,3,2,1,0:T(8,128)S(1)}, f32[1,1,1,1,104,640]{5,4,3,2,1,0:T(8,128)S(1)}, u32[]{:S(2)}, u32[]{:S(2)}) collective-permute-start(f32[1,1,1,1,104,640]{5,4,3,2,1,0:T(8,128)S(1)} %slice_add_fusion.11), channel_id=1, source_target_pairs={{0,1},{1,0},{2,3},{3,2},{4,5},{5,4},{6,7},{7,6},{8,9},{9,8},{10,11... | collective-permute-start | bytes 798728 | tf_op jit(solution)/shard_map/ppermute | solution.py:235
  241.9 14.3 %collective-permute-start.21 = (f32[1,1,1,1,104,640]{5,4,3,2,1,0:T(8,128)S(1)}, f32[1,1,1,1,104,640]{5,4,3,2,1,0:T(8,128)S(1)}, u32[]{:S(2)}, u32[]{:S(2)}) collective-permute-start(f32[1,1,1,1,104,640]{5,4,3,2,1,0:T(8,128)S(1)} %slice_add_fusion.8), channel_id=1, source_target_pairs={{0,1},{1,0},{2,3},{3,2},{4,5},{5,4},{6,7},{7,6},{8,9},{9,8},{10,11... | collective-permute-start | bytes 798728 | tf_op jit(solution)/shard_map/ppermute | solution.py:235
  (15 other events, 36.3 us)
Sparse Core Ops, SparseCore 0:
  10.2 104.4 all-gather.1

commit v4 on v3

--- a/solution.py
+++ b/solution.py
@@ -310,7 +310,7 @@
             weight, masked_cot, (((1,), (1,)), ((), ())), preferred_element_type=jnp.float32
         ).astype(jnp.bfloat16)
 
-    cuts = (0, heads * 5 // 13, heads * 11 // 13, heads)
+    cuts = (0, heads * 7 // 13, heads)
 
     def backward(grad_t, index, before):
         return attention_backward(
@@ -347,26 +347,26 @@
     second = part_of(second, last, 0) + s_in
     third = middle(part_of(third, near, 0) + t_in)
     fifth = part_of(fifth, x, 0) + f_in
-    (o_in, s_in, t_in, f_in), grad_projected = together(
+    (o_in, s_in, t_in, f_in), work_out = together(
         [
             (part_of(own, x, 1), x),
             (second, -1),
             (part_of(third, last, 1), last),
             (fifth, -1),
         ],
-        (grad_t, grad_projected),
-        lambda held: backward(held[0], 2, held[1]),
+        (attn_t, full_weight),
+        lambda held: lax.dot_general(
+            held[0], held[1], (((0,), (0,)), ((), ())), preferred_element_type=jnp.float32
+        ).astype(jnp.bfloat16),
     )
     own = part_of(own, x, 0) + o_in
     second = second + s_in
     third = part_of(third, last, 0) + t_in
     fifth = fifth + f_in
-    (o_in, t_in), work_out = together(
+    (o_in, t_in), _ = together(
         [(own, -1), (third, -1)],
-        (attn_t, full_weight),
-        lambda held: lax.dot_general(
-            held[0], held[1], (((0,), (0,)), ((), ())), preferred_element_type=jnp.float32
-        ).astype(jnp.bfloat16),
+        (),
+        nothing,
     )
     pieces = [
         jnp.where(row_side == 0, own, o_in),

time: 265 us -> 258 us (0.974)
  waiting for transfers between devices: 62.6 us -> 68.3 us
  other arithmetic: 13.4 us -> 7.82 us
  local copies, waits for them, and re-layouts: 17.7 us -> 13 us
  matrix products: 58.2 us -> 54.5 us
    ppermute x5, waiting for transfers between devices: 0.01 us -> 9.65 us  [across(): return lax.ppermute(array, 'dp', [(i, i ^ 1) for i in range(pair)])]
    ppermute x17, waiting for transfers between devices: 62.5 us -> 58.6 us  [across(): lax.ppermute(array, 'fsdp', [(i, i ^ 1 << bit) for i in range(devices)])]
    dot_general x10, matrix products: 33 us -> 29.2 us  [product(): return jnp.dot(left, cot, preferred_element_type=jnp.float32)]
    slice x12, local copies, waits for them, and re-layouts: 6.52 us -> 3.28 us  [part_of(): return lax.slice_in_dim(array, which, which + 1, axis=bit)]
    unnamed x55 -> x43, local copies, waits for them, and re-layouts: 10.5 us -> 9.06 us
    pallas_call x3 -> x2, Pallas kernels: 56.2 us -> 55.1 us  [attention_backward(): pl.pallas_call(kernel, grid_spec=pltpu.PrefetchScalarGridSpec(num_scalar_...]
  transfers between devices with their start and end apart: 23 -> 23, of which waited for: 5 -> 6; matrix products, arithmetic and copies ran while one was open for 31% -> 27% of each run, Pallas kernels for 28% -> 29%
where the time goes in v4:
time: 258 us; the launch traced here: 255 us
  Pallas kernels  73.8 us (29%)
  waiting for transfers between devices  68.3 us (26%)
  matrix products  54.5 us (21%)
  starting transfers between devices  22.8 us (9%)
  between operations  14.6 us (6%)
  local copies, waits for them, and re-layouts  13 us (5%)
  other arithmetic  7.82 us (3%)
    ppermute x17, waiting for transfers between devices, across(): lax.ppermute(array, 'fsdp', [(i, i ^ 1 << bit) for i in range(devices)])  58.6 us
    pallas_call x2, Pallas kernels, attention_backward(): pl.pallas_call(kernel, grid_spec=pltpu.PrefetchScalarGridSpec(num_scalar_...  55.1 us
    dot_general x10, matrix products, product(): return jnp.dot(left, cot, preferred_element_type=jnp.float32)  29.2 us
    pallas_call x1, Pallas kernels, attention_forward(): pl.pallas_call(forward_kernel, grid_spec=pltpu.PrefetchScalarGridSpec(num...  18.7 us
    ppermute x17, starting transfers between devices, across(): lax.ppermute(array, 'fsdp', [(i, i ^ 1 << bit) for i in range(devices)])  16 us
    dot_general x1, matrix products, grad_of(): lax.dot_general(weight, masked_cot, (((1,), (1,)), ((), ())), preferred_e...  12.6 us
    dot_general x1, matrix products, body(): lax.dot_general(held[0], held[1], (((0,), (0,)), ((), ())), preferred_ele...  12.6 us
    ppermute x5, waiting for transfers between devices, across(): return lax.ppermute(array, 'dp', [(i, i ^ 1) for i in range(pair)])  9.65 us
  transfers between devices with their start and end apart: 23, of which 6 were waited for; matrix products, arithmetic and copies ran while one was open for 27% of the time, Pallas kernels for 29%

profile of v4, /device:TPU:0, one launch (start us, length us, event | category | flops | bytes accessed | tf_op | source)
XLA Modules:
  0.0 254.8 jit_solution(7752917164869213813)
XLA Ops:
  7.3 2.2 convert_element_type.29
  11.0 2.4 fusion.17
  13.6 18.7 %shard_map.94 = bf16[1664,640]{1,0:T(8,128)(2,1)S(1)} custom-call(s32[2]{0:T(128)S(1)} %copy-done, bf16[640,4992]{1,0:T(8,128)(2,1)} %refs_3_.1, bf16[640,4992]{1,0:T(8,128)(2,1)} %refs_3_.1, bf16[640,4992]{1,0:T(8,128)(2,1)} %refs_3_.1, f32[640,128]{1,0:T(8,128)S(1)} %get-tuple-element.111.cos_ref.refs_5_, f32[640,128]{1,0:T(8,128)S(1)} %get-tuple-element.112.sin_ref.refs_6_), custom_call_target="tpu_custom_call" | custom-call | flops 4089446400 | bytes 8519680 | tf_op jit(solution)/shard_map/pallas_call | solution.py:144
  38.3 2.7 %fusion.6 = f32[832,640]{1,0:T(8,128)} fusion(bf16[832,640]{1,0:T(8,128)(2,1)S(1)} %get-tuple-element.90, bf16[640,3200]{1,0:T(8,128)(2,1)S(1)} %broadcast_multiply_fusion), kind=kOutput, calls=%fused_computation.18 | convolution fusion | flops 681574400 | bytes 4014080 | tf_op jit(solution)/shard_map/dot_general | solution.py:267
  41.4 2.5 fusion.3
  43.9 2.5 fusion
  46.8 3.9 %fusion.9 = f32[832,640]{1,0:T(8,128)} fusion(bf16[832,640]{1,0:T(8,128)(2,1)} %copy-done.13, bf16[640,3200]{1,0:T(8,128)(2,1)} %copy-done.1, s32[]{:T(128)S(6)} %select_n.118), kind=kOutput, calls=%fused_computation.21 | convolution fusion | flops 681574400 | bytes 4014084 | tf_op jit(solution)/shard_map/dot_general | solution.py:267
  50.7 3.3 %fusion.12 = f32[832,640]{1,0:T(8,128)S(1)} fusion(bf16[832,640]{1,0:T(8,128)(2,1)} %copy-done.13, bf16[640,3200]{1,0:T(8,128)(2,1)} %copy-done.1, s32[]{:T(128)S(6)} %select_n.109), kind=kOutput, calls=%fused_computation.24 | convolution fusion | flops 681574400 | bytes 4014084 | tf_op jit(solution)/shard_map/dot_general | solution.py:267
  54.6 3.0 %convolution_add_fusion.2 = f32[832,640]{1,0:T(8,128)S(1)} fusion(f32[832,640]{1,0:T(8,128)} %collective-permute-done.2, bf16[832,640]{1,0:T(8,128)(2,1)} %get-tuple-element.89, bf16[640,3200]{1,0:T(8,128)(2,1)S(1)} %copy-done.2), kind=kOutput, calls=%fused_computation.5 | convolution fusion | flops 682106880 | bytes 6144000 | tf_op jit(solution)/shard_map/dot_general | solution.py:267
  57.7 3.0 %convolution_add_fusion.1 = f32[832,640]{1,0:T(8,128)S(1)} fusion(f32[832,640]{1,0:T(8,128)} %collective-permute-done.3, bf16[832,640]{1,0:T(8,128)(2,1)} %get-tuple-element.89, bf16[640,3200]{1,0:T(8,128)(2,1)S(1)} %copy-done.2), kind=kOutput, calls=%fused_computation.4 | convolution fusion | flops 682106880 | bytes 6144000 | tf_op jit(solution)/shard_map/dot_general | solution.py:267
  60.8 3.1 %convolution_add_fusion = f32[832,640]{1,0:T(8,128)S(1)} fusion(f32[832,640]{1,0:T(8,128)} %collective-permute-done.4, bf16[832,640]{1,0:T(8,128)(2,1)} %get-tuple-element.89, bf16[640,3200]{1,0:T(8,128)(2,1)S(1)} %copy-done.2), kind=kOutput, calls=%fused_computation.3 | convolution fusion | flops 682106880 | bytes 6144000 | tf_op jit(solution)/shard_map/dot_general | solution.py:267
  64.0 3.0 %convolution_add_fusion.3 = f32[832,640]{1,0:T(8,128)S(1)} fusion(f32[832,640]{1,0:T(8,128)} %collective-permute-done.1, bf16[832,640]{1,0:T(8,128)(2,1)} %get-tuple-element.89, bf16[640,3200]{1,0:T(8,128)(2,1)S(1)} %copy-done.2, s32[]{:T(128)S(6)} %select_n.118), kind=kOutput, calls=%fused_computation.6 | convolution fusion | flops 682106880 | bytes 6144004 | tf_op jit(solution)/shard_map/dot_general | solution.py:267
  67.0 2.6 %collective-permute-start.5 = (f32[1,2,2,2,104,640]{5,4,3,2,1,0:T(8,128)S(1)}, f32[1,2,2,2,104,640]{5,4,3,2,1,0:T(8,128)S(1)}, u32[]{:S(2)}, u32[]{:S(2)}) collective-permute-start(f32[1,2,2,2,104,640]{5,4,3,2,1,0:T(8,128)S(1)} %bitcast.36), channel_id=1, source_target_pairs={{0,1},{1,0},{2,3},{3,2},{4,5},{5,4},{6,7},{7,6},{8,9},{9,8},{10,11... | collective-permute-start | bytes 6389768 | tf_op jit(solution)/shard_map/ppermute | solution.py:235
  69.6 1.5 collective-permute-start.6
  71.7 1.6 collective-permute-start.8
  73.2 2.3 convolution_add_fusion.4
  75.6 29.5 %collective-permute-done.6 = f32[1,1,2,2,104,640]{5,4,3,2,1,0:T(8,128)S(1)} collective-permute-done((f32[1,1,2,2,104,640]{5,4,3,2,1,0:T(8,128)S(1)}, f32[1,1,2,2,104,640]{5,4,3,2,1,0:T(8,128)S(1)}, u32[]{:S(2)}, u32[]{:S(2)}) %collective-permute-start.6) | collective-permute-done | bytes 1064992 | tf_op jit(solution)/shard_map/ppermute | solution.py:236
  105.1 22.4 %collective-permute-done.7 = f32[1,1,2,2,104,640]{5,4,3,2,1,0:T(8,128)S(1)} collective-permute-done((f32[1,1,2,2,104,640]{5,4,3,2,1,0:T(8,128)S(1)}, f32[1,1,2,2,104,640]{5,4,3,2,1,0:T(8,128)S(1)}, u32[]{:S(2)}, u32[]{:S(2)}) %collective-permute-start.7) | collective-permute-done | bytes 1064992 | tf_op jit(solution)/shard_map/ppermute | solution.py:236
  132.9 1.6 collective-permute-start.9
  135.0 2.4 collective-permute-start.11
  137.4 12.6 %convolution_convert_fusion.1.g_ref.refs_4_ = bf16[1664,640]{1,0:T(8,128)(2,1)S(1)} fusion(bf16[1664,3200]{1,0:T(8,128)(2,1)} %all-gather.2.cloned.1.call-done, bf16[640,3200]{1,0:T(8,128)(2,1)} %copy-done.1), kind=kOutput, calls=%fused_computation.1 | convolution fusion | flops 6816808960 | bytes 16875520 | tf_op jit(solution)/shard_map/dot_general | solution.py:309
  150.0 29.6 %shard_map.95.refs_7_ = bf16[640,4992]{1,0:T(8,128)(2,1)} custom-call(s32[2]{0:T(128)S(1)} %copy-done, bf16[640,4992]{1,0:T(8,128)(2,1)} %refs_3_.1, bf16[640,4992]{1,0:T(8,128)(2,1)} %refs_3_.1, bf16[640,4992]{1,0:T(8,128)(2,1)} %refs_3_.1, bf16[1664,640]{1,0:T(8,128)(2,1)S(1)} %convolution_convert_fusion.1.g_ref.refs_4_, ...), custom_call_target="tpu_custom_call" | custom-call | flops 25690112000 | bytes 8028160 | tf_op jit(solution)/shard_map/pallas_call | solution.py:196
  179.6 1.5 collective-permute-done.10
  182.9 2.5 collective-permute-start.12
  185.8 2.4 collective-permute-start.14
  188.8 25.5 %shard_map.96 = bf16[640,4992]{1,0:T(8,128)(2,1)} custom-call(s32[2]{0:T(128)S(1)} %copy-done, bf16[640,4992]{1,0:T(8,128)(2,1)} %refs_3_.1, bf16[640,4992]{1,0:T(8,128)(2,1)} %refs_3_.1, bf16[640,4992]{1,0:T(8,128)(2,1)} %refs_3_.1, bf16[1664,640]{1,0:T(8,128)(2,1)S(1)} %convolution_convert_fusion.1.g_ref.refs_4_, ...), custom_call_target="tpu_custom_call", output_to_operand_aliasing={{}: (7, {})} | custom-call | flops 22020096000 | bytes 6881280 | tf_op jit(solution)/shard_map/pallas_call | solution.py:196
  214.3 5.1 %collective-permute-done.13 = f32[1,1,1,1,104,640]{5,4,3,2,1,0:T(8,128)S(1)} collective-permute-done((f32[1,1,1,1,104,640]{5,4,3,2,1,0:T(8,128)S(1)}, f32[1,1,1,1,104,640]{5,4,3,2,1,0:T(8,128)S(1)}, u32[]{:S(2)}, u32[]{:S(2)}) %collective-permute-start.13) | collective-permute-done | bytes 266272 | tf_op jit(solution)/shard_map/ppermute | solution.py:236
  220.2 1.7 collective-permute-start.17
  222.2 12.6 %convolution_convert_fusion = bf16[640,3200]{1,0:T(8,128)(2,1)} fusion(bf16[1664,640]{1,0:T(8,128)(2,1)S(1)} %shard_map.94, bf16[1664,3200]{1,0:T(8,128)(2,1)} %all-gather.2.cloned.1.call-done), kind=kOutput, calls=%fused_computation | convolution fusion | flops 6817792000 | bytes 16875520 | tf_op jit(solution)/shard_map/dot_general | solution.py:358
  234.9 1.8 collective-permute-start.20
  237.0 6.8 %collective-permute-done.20 = f32[1,1,1,1,104,640]{5,4,3,2,1,0:T(8,128)S(1)} collective-permute-done((f32[1,1,1,1,104,640]{5,4,3,2,1,0:T(8,128)S(1)}, f32[1,1,1,1,104,640]{5,4,3,2,1,0:T(8,128)S(1)}, u32[]{:S(2)}, u32[]{:S(2)}) %collective-permute-start.20) | collective-permute-done | bytes 266272 | tf_op jit(solution)/shard_map/ppermute | solution.py:235
  243.8 2.9 %collective-permute-done.21 = f32[1,1,1,1,104,640]{5,4,3,2,1,0:T(8,128)S(1)} collective-permute-done((f32[1,1,1,1,104,640]{5,4,3,2,1,0:T(8,128)S(1)}, f32[1,1,1,1,104,640]{5,4,3,2,1,0:T(8,128)S(1)}, u32[]{:S(2)}, u32[]{:S(2)}) %collective-permute-start.21) | collective-permute-done | bytes 266272 | tf_op jit(solution)/shard_map/ppermute | solution.py:235
  (111 shorter events, 21.1 us)
Async XLA Ops:
  7.2 3.8 %copy-start.15 = (f32[64]{0:T(128)S(1)}, f32[64]{0:T(128)}, u32[]{:S(2)}) copy-start(f32[64]{0:T(128)} %constant.97.clone) | copy-start | bytes 772
  7.2 3.8 %copy-start.16 = (pred[64]{0:T(512)(128)(4,1)S(1)}, pred[64]{0:T(512)(128)(4,1)}, u32[]{:S(2)}) copy-start(pred[64]{0:T(512)(128)(4,1)} %constant.101) | copy-start | bytes 196
  7.2 3.8 %copy-start.17 = (pred[64]{0:T(512)(128)(4,1)S(1)}, pred[64]{0:T(512)(128)(4,1)}, u32[]{:S(2)}) copy-start(pred[64]{0:T(512)(128)(4,1)} %constant.100) | copy-start | bytes 196
  7.2 125.6 %all-gather.2.cloned.1.call-start = ((), (), s32[]{:S(2)}) async-start(), calls=%async_computation | async-start | bytes 11315200 | tf_op jit(solution)/shard_map/all_gather | solution.py:254
  32.3 5.5 %copy-start.11 = (bf16[640,3200]{1,0:T(8,128)(2,1)S(1)}, bf16[640,3200]{1,0:T(8,128)(2,1)}, u32[]{:S(2)}) copy-start(bf16[640,3200]{1,0:T(8,128)(2,1)} %param.8) | copy-start | bytes 12288004
  37.8 6.1 %copy-start.13 = (bf16[832,640]{1,0:T(8,128)(2,1)}, bf16[832,640]{1,0:T(8,128)(2,1)S(1)}, u32[]{:S(2)}) copy-start(bf16[832,640]{1,0:T(8,128)(2,1)S(1)} %get-tuple-element.90) | copy-start | bytes 3194884
  38.3 5.6 %copy-start.1 = (bf16[640,3200]{1,0:T(8,128)(2,1)}, bf16[640,3200]{1,0:T(8,128)(2,1)S(1)}, u32[]{:S(2)}) copy-start(bf16[640,3200]{1,0:T(8,128)(2,1)S(1)} %broadcast_multiply_fusion) | copy-start | bytes 12288004
  40.9 13.6 %collective-permute-start.2 = (f32[832,640]{1,0:T(8,128)}, f32[832,640]{1,0:T(8,128)}, u32[]{:S(2)}, u32[]{:S(2)}) collective-permute-start(f32[832,640]{1,0:T(8,128)} %fusion.6), channel_id=1, source_target_pairs={{0,2},{2,0},{4,6},{6,4},{8,10},{10,8},{12,14},{14,12},{16,18},{18,... | collective-permute-start | bytes 6389768 | tf_op jit(solution)/shard_map/ppermute | solution.py:236
  43.8 13.8 %collective-permute-start.3 = (f32[832,640]{1,0:T(8,128)}, f32[832,640]{1,0:T(8,128)}, u32[]{:S(2)}, u32[]{:S(2)}) collective-permute-start(f32[832,640]{1,0:T(8,128)} %fusion.3), channel_id=1, source_target_pairs={{0,2},{2,0},{4,6},{6,4},{8,10},{10,8},{12,14},{14,12},{16,18},{18,... | collective-permute-start | bytes 6389768 | tf_op jit(solution)/shard_map/ppermute | solution.py:236
  46.3 14.4 %collective-permute-start.4 = (f32[832,640]{1,0:T(8,128)}, f32[832,640]{1,0:T(8,128)}, u32[]{:S(2)}, u32[]{:S(2)}) collective-permute-start(f32[832,640]{1,0:T(8,128)} %fusion), channel_id=1, source_target_pairs={{0,2},{2,0},{4,6},{6,4},{8,10},{10,8},{12,14},{14,12},{16,18},{18,... | collective-permute-start | bytes 6389768 | tf_op jit(solution)/shard_map/ppermute | solution.py:236
  50.7 13.3 %collective-permute-start.1 = (f32[832,640]{1,0:T(8,128)}, f32[832,640]{1,0:T(8,128)}, u32[]{:S(2)}, u32[]{:S(2)}) collective-permute-start(f32[832,640]{1,0:T(8,128)} %fusion.9), channel_id=1, source_target_pairs={{0,2},{2,0},{4,6},{6,4},{8,10},{10,8},{12,14},{14,12},{16,18},{18,... | collective-permute-start | bytes 6389768 | tf_op jit(solution)/shard_map/ppermute | solution.py:236
  50.7 3.8 %copy-start.2 = (bf16[640,3200]{1,0:T(8,128)(2,1)S(1)}, bf16[640,3200]{1,0:T(8,128)(2,1)}, u32[]{:S(2)}) copy-start(bf16[640,3200]{1,0:T(8,128)(2,1)} %copy-done.1) | copy-start | bytes 12288004
  54.0 19.2 %collective-permute-start = (f32[832,640]{1,0:T(8,128)S(1)}, f32[832,640]{1,0:T(8,128)S(1)}, u32[]{:S(2)}, u32[]{:S(2)}) collective-permute-start(f32[832,640]{1,0:T(8,128)S(1)} %fusion.12), channel_id=1, source_target_pairs={{0,2},{2,0},{4,6},{6,4},{8,10},{10,8},{12,14},{14,12},{16,18},{18,... | collective-permute-start | bytes 6389768 | tf_op jit(solution)/shard_map/ppermute | solution.py:236
  67.0 60.5 %collective-permute-start.5 = (f32[1,2,2,2,104,640]{5,4,3,2,1,0:T(8,128)S(1)}, f32[1,2,2,2,104,640]{5,4,3,2,1,0:T(8,128)S(1)}, u32[]{:S(2)}, u32[]{:S(2)}) collective-permute-start(f32[1,2,2,2,104,640]{5,4,3,2,1,0:T(8,128)S(1)} %bitcast.36), channel_id=1, source_target_pairs={{0,1},{1,0},{2,3},{3,2},{4,5},{5,4},{6,7},{7,6},{8,9},{9,8},{10,11... | collective-permute-start | bytes 6389768 | tf_op jit(solution)/shard_map/ppermute | solution.py:235
  69.6 35.5 %collective-permute-start.6 = (f32[1,1,2,2,104,640]{5,4,3,2,1,0:T(8,128)S(1)}, f32[1,1,2,2,104,640]{5,4,3,2,1,0:T(8,128)S(1)}, u32[]{:S(2)}, u32[]{:S(2)}) collective-permute-start(f32[1,1,2,2,104,640]{5,4,3,2,1,0:T(8,128)S(1)} %slice.107), channel_id=1, source_target_pairs={{0,4},{2,6},{4,0},{6,2},{8,12},{10,14},{12,8},{14,10},{16,20},{18,... | collective-permute-start | bytes 3194888 | tf_op jit(solution)/shard_map/ppermute | solution.py:236
  71.1 56.4 %collective-permute-start.7 = (f32[1,1,2,2,104,640]{5,4,3,2,1,0:T(8,128)S(1)}, f32[1,1,2,2,104,640]{5,4,3,2,1,0:T(8,128)S(1)}, u32[]{:S(2)}, u32[]{:S(2)}) collective-permute-start(f32[1,1,2,2,104,640]{5,4,3,2,1,0:T(8,128)S(1)} %slice.108), channel_id=1, source_target_pairs={{0,4},{2,6},{4,0},{6,2},{8,12},{10,14},{12,8},{14,10},{16,20},{18,... | collective-permute-start | bytes 3194888 | tf_op jit(solution)/shard_map/ppermute | solution.py:236
  71.7 55.9 %collective-permute-start.8 = (f32[1,2,1,2,104,640]{5,4,3,2,1,0:T(8,128)S(1)}, f32[1,2,1,2,104,640]{5,4,3,2,1,0:T(8,128)S(1)}, u32[]{:S(2)}, u32[]{:S(2)}) collective-permute-start(f32[1,2,1,2,104,640]{5,4,3,2,1,0:T(8,128)S(1)} %slice.109), channel_id=1, source_target_pairs={{0,8},{2,10},{4,12},{6,14},{8,0},{10,2},{12,4},{14,6},{16,24},{18,... | collective-permute-start | bytes 3194888 | tf_op jit(solution)/shard_map/ppermute | solution.py:236
  132.9 48.2 %collective-permute-start.9 = (f32[1,2,1,2,104,640]{5,4,3,2,1,0:T(8,128)}, f32[1,2,1,2,104,640]{5,4,3,2,1,0:T(8,128)S(1)}, u32[]{:S(2)}, u32[]{:S(2)}) collective-permute-start(f32[1,2,1,2,104,640]{5,4,3,2,1,0:T(8,128)} %slice.111), channel_id=1, source_target_pairs={{0,8},{2,10},{4,12},{6,14},{8,0},{10,2},{12,4},{14,6},{16,24},{18,... | collective-permute-start | bytes 3194888 | tf_op jit(solution)/shard_map/ppermute | solution.py:236
  134.4 46.7 %collective-permute-start.10 = (f32[1,1,1,2,104,640]{5,4,3,2,1,0:T(8,128)}, f32[1,1,1,2,104,640]{5,4,3,2,1,0:T(8,128)S(1)}, u32[]{:S(2)}, u32[]{:S(2)}) collective-permute-start(f32[1,1,1,2,104,640]{5,4,3,2,1,0:T(8,128)} %slice.113), channel_id=1, source_target_pairs={{0,8},{2,10},{4,12},{6,14},{8,0},{10,2},{12,4},{14,6},{16,24},{18,... | collective-permute-start | bytes 1597448 | tf_op jit(solution)/shard_map/ppermute | solution.py:236
  135.0 46.1 %collective-permute-start.11 = (f32[1,2,1,1,104,640]{5,4,3,2,1,0:T(8,128)}, f32[1,2,1,1,104,640]{5,4,3,2,1,0:T(8,128)S(1)}, u32[]{:S(2)}, u32[]{:S(2)}) collective-permute-start(f32[1,2,1,1,104,640]{5,4,3,2,1,0:T(8,128)} %slice.115), channel_id=1, source_target_pairs={{0,16},{2,18},{4,20},{6,22},{8,24},{10,26},{12,28},{14,30},{16,0},... | collective-permute-start | bytes 1597448 | tf_op jit(solution)/shard_map/ppermute | solution.py:236
  150.0 31.1 %copy-start.4 = (f32[1,2,2,2,104,640]{5,4,3,2,1,0:T(8,128)S(1)}, f32[1,2,2,2,104,640]{5,4,3,2,1,0:T(8,128)}, u32[]{:S(2)}) copy-start(f32[1,2,2,2,104,640]{5,4,3,2,1,0:T(8,128)} %copy-done.3) | copy-start | bytes 6389764
  182.9 36.6 %collective-permute-start.12 = (f32[1,2,1,1,104,640]{5,4,3,2,1,0:T(8,128)S(1)}, f32[1,2,1,1,104,640]{5,4,3,2,1,0:T(8,128)S(1)}, u32[]{:S(2)}, u32[]{:S(2)}) collective-permute-start(f32[1,2,1,1,104,640]{5,4,3,2,1,0:T(8,128)S(1)} %slice.117), channel_id=1, source_target_pairs={{0,16},{2,18},{4,20},{6,22},{8,24},{10,26},{12,28},{14,30},{16,0},... | collective-permute-start | bytes 1597448 | tf_op jit(solution)/shard_map/ppermute | solution.py:236
  185.3 34.2 %collective-permute-start.13 = (f32[1,1,1,1,104,640]{5,4,3,2,1,0:T(8,128)S(1)}, f32[1,1,1,1,104,640]{5,4,3,2,1,0:T(8,128)S(1)}, u32[]{:S(2)}, u32[]{:S(2)}) collective-permute-start(f32[1,1,1,1,104,640]{5,4,3,2,1,0:T(8,128)S(1)} %slice.119), channel_id=1, source_target_pairs={{0,16},{2,18},{4,20},{6,22},{8,24},{10,26},{12,28},{14,30},{16,0},... | collective-permute-start | bytes 798728 | tf_op jit(solution)/shard_map/ppermute | solution.py:236
  185.8 33.6 %collective-permute-start.14 = (f32[1,1,1,2,104,640]{5,4,3,2,1,0:T(8,128)S(1)}, f32[1,1,1,2,104,640]{5,4,3,2,1,0:T(8,128)S(1)}, u32[]{:S(2)}, u32[]{:S(2)}) collective-permute-start(f32[1,1,1,2,104,640]{5,4,3,2,1,0:T(8,128)S(1)} %slice.121), channel_id=1, source_target_pairs={{0,8},{2,10},{4,12},{6,14},{8,0},{10,2},{12,4},{14,6},{16,24},{18,... | collective-permute-start | bytes 1597448 | tf_op jit(solution)/shard_map/ppermute | solution.py:236
  188.3 31.2 %collective-permute-start.15 = (f32[1,1,1,1,104,640]{5,4,3,2,1,0:T(8,128)S(1)}, f32[1,1,1,1,104,640]{5,4,3,2,1,0:T(8,128)S(1)}, u32[]{:S(2)}, u32[]{:S(2)}) collective-permute-start(f32[1,1,1,1,104,640]{5,4,3,2,1,0:T(8,128)S(1)} %slice.123), channel_id=1, source_target_pairs={{0,4},{2,6},{4,0},{6,2},{8,12},{10,14},{12,8},{14,10},{16,20},{18,... | collective-permute-start | bytes 798728 | tf_op jit(solution)/shard_map/ppermute | solution.py:236
  214.3 5.3 %copy-start.6 = (f32[1,1,2,2,104,640]{5,4,3,2,1,0:T(8,128)S(1)}, f32[1,1,2,2,104,640]{5,4,3,2,1,0:T(8,128)}, u32[]{:S(2)}) copy-start(f32[1,1,2,2,104,640]{5,4,3,2,1,0:T(8,128)} %copy-done.5) | copy-start | bytes 3194884
  219.8 15.1 %collective-permute-start.16 = (f32[1,1,1,1,104,640]{5,4,3,2,1,0:T(8,128)S(1)}, f32[1,1,1,1,104,640]{5,4,3,2,1,0:T(8,128)S(1)}, u32[]{:S(2)}, u32[]{:S(2)}) collective-permute-start(f32[1,1,1,1,104,640]{5,4,3,2,1,0:T(8,128)S(1)} %slice.124), channel_id=1, source_target_pairs={{0,4},{2,6},{4,0},{6,2},{8,12},{10,14},{12,8},{14,10},{16,20},{18,... | collective-permute-start | bytes 798728 | tf_op jit(solution)/shard_map/ppermute | solution.py:236
  220.2 14.7 %collective-permute-start.17 = (f32[1,1,1,1,104,640]{5,4,3,2,1,0:T(8,128)S(1)}, f32[1,1,1,1,104,640]{5,4,3,2,1,0:T(8,128)S(1)}, u32[]{:S(2)}, u32[]{:S(2)}) collective-permute-start(f32[1,1,1,1,104,640]{5,4,3,2,1,0:T(8,128)S(1)} %slice_add_fusion.11), channel_id=1, source_target_pairs={{0,1},{1,0},{2,3},{3,2},{4,5},{5,4},{6,7},{7,6},{8,9},{9,8},{10,11... | collective-permute-start | bytes 798728 | tf_op jit(solution)/shard_map/ppermute | solution.py:235
  221.9 13.0 %collective-permute-start.18 = (f32[1,1,1,1,104,640]{5,4,3,2,1,0:T(8,128)S(1)}, f32[1,1,1,1,104,640]{5,4,3,2,1,0:T(8,128)S(1)}, u32[]{:S(2)}, u32[]{:S(2)}) collective-permute-start(f32[1,1,1,1,104,640]{5,4,3,2,1,0:T(8,128)S(1)} %slice.127), channel_id=1, source_target_pairs={{0,16},{2,18},{4,20},{6,22},{8,24},{10,26},{12,28},{14,30},{16,0},... | collective-permute-start | bytes 798728 | tf_op jit(solution)/shard_map/ppermute | solution.py:236
  221.9 13.0 %collective-permute-start.19 = (f32[1,1,1,1,104,640]{5,4,3,2,1,0:T(8,128)S(1)}, f32[1,1,1,1,104,640]{5,4,3,2,1,0:T(8,128)S(1)}, u32[]{:S(2)}, u32[]{:S(2)}) collective-permute-start(f32[1,1,1,1,104,640]{5,4,3,2,1,0:T(8,128)S(1)} %slice_add_fusion.10), channel_id=1, source_target_pairs={{0,1},{1,0},{2,3},{3,2},{4,5},{5,4},{6,7},{7,6},{8,9},{9,8},{10,11... | collective-permute-start | bytes 798728 | tf_op jit(solution)/shard_map/ppermute | solution.py:235
  234.9 8.9 %collective-permute-start.20 = (f32[1,1,1,1,104,640]{5,4,3,2,1,0:T(8,128)S(1)}, f32[1,1,1,1,104,640]{5,4,3,2,1,0:T(8,128)S(1)}, u32[]{:S(2)}, u32[]{:S(2)}) collective-permute-start(f32[1,1,1,1,104,640]{5,4,3,2,1,0:T(8,128)S(1)} %slice_add_fusion.9), channel_id=1, source_target_pairs={{0,1},{1,0},{2,3},{3,2},{4,5},{5,4},{6,7},{7,6},{8,9},{9,8},{10,11... | collective-permute-start | bytes 798728 | tf_op jit(solution)/shard_map/ppermute | solution.py:235
  236.7 10.0 %collective-permute-start.21 = (f32[1,1,1,1,104,640]{5,4,3,2,1,0:T(8,128)S(1)}, f32[1,1,1,1,104,640]{5,4,3,2,1,0:T(8,128)S(1)}, u32[]{:S(2)}, u32[]{:S(2)}) collective-permute-start(f32[1,1,1,1,104,640]{5,4,3,2,1,0:T(8,128)S(1)} %slice_add_fusion.8), channel_id=1, source_target_pairs={{0,1},{1,0},{2,3},{3,2},{4,5},{5,4},{6,7},{7,6},{8,9},{9,8},{10,11... | collective-permute-start | bytes 798728 | tf_op jit(solution)/shard_map/ppermute | solution.py:235
  (9 other events, 15.0 us)
Sparse Core Ops, SparseCore 0:
  10.2 107.6 all-gather.1
